TPU v7x, 32 devices: a whole 2x2x4 slice. The times are simulated.
32 devices in a mesh: dp: 2 (over y), seq: 16 (over z, x, core).
Axes of the slice: x: 2, y: 2, z: 4, core: 2. Of those that a mesh axis runs over, the one named last changes fastest.
Arguments:
- tokens: bfloat16 [4, 2048, 768], P('dp', 'seq'), may hold values from -6 to 6
- segments: int32 [4, 2048], P('dp', 'seq'), may hold values from -1 to 3, as said below
- query_route: int32 [4, 256], P('dp'), may hold values from 0 to 2047, as said below
- kv_route: int32 [4, 256], P('dp'), may hold values from 0 to 2047, as said below
- ffn_route: int32 [4, 256], P('dp', 'seq'), may hold values from 0 to 2047, as said below
- grad_out: bfloat16 [4, 2048, 768], P('dp', 'seq'), may hold values from -6 to 6
- attn_gain: float32 [768], replicated, may hold values from 0.5 to 1.5
- light_qkv: bfloat16 [768, 2304], replicated, may hold values from -0.21875 to 0.21875
- light_out: bfloat16 [768, 768], replicated, may hold values from -2.5 to 2.5
- heavy_q: bfloat16 [768, 768], replicated, may hold values from -0.21875 to 0.21875
- heavy_kv: bfloat16 [768, 1536], replicated, may hold values from -0.21875 to 0.21875
- heavy_out: bfloat16 [768, 768], replicated, may hold values from -6 to 6
- route_query: bfloat16 [768], replicated, may hold values from -0.21875 to 0.21875
- ffn_gain: float32 [768], replicated, may hold values from 0.5 to 1.5
- light_gate_up: bfloat16 [768, 2048], replicated, may hold values from -0.21875 to 0.21875
- light_down: bfloat16 [1024, 768], replicated, may hold values from -0.1875 to 0.1875
- heavy_gate_up: bfloat16 [768, 8192], replicated, may hold values from -0.21875 to 0.21875
- heavy_down: bfloat16 [4096, 768], replicated, may hold values from -0.09375 to 0.09375
- route_ffn: bfloat16 [768], replicated, may hold values from -0.21875 to 0.21875
Outputs:
- outputs: bfloat16 [4, 2048, 768], P('dp', 'seq')
- grad_tokens: bfloat16 [4, 2048, 768], P('dp', 'seq')
- grad_attn_gain: float32 [768], P('seq')
- grad_light_qkv: float32 [768, 2304], P('seq', 'dp')
- grad_light_out: float32 [768, 768], P('seq', 'dp')
- grad_heavy_q: float32 [768, 768], P('seq', 'dp')
- grad_heavy_kv: float32 [768, 1536], P('seq', 'dp')
- grad_heavy_out: float32 [768, 768], P('seq', 'dp')
- grad_route_query: float32 [768], P('seq')
- grad_ffn_gain: float32 [768], P('seq')
- grad_light_gate_up: float32 [768, 2048], P('seq', 'dp')
- grad_light_down: float32 [1024, 768], P('seq', 'dp')
- grad_heavy_gate_up: float32 [768, 8192], P('seq', 'dp')
- grad_heavy_down: float32 [4096, 768], P('seq', 'dp')
- grad_route_ffn: float32 [768], P('seq')
- rms_stats: float32 [5], replicated
Inputs may be any that keep to these rules, and one draw needn't show every extreme that they name: `segments`: never falls along a row; -1 only fills the end of the last row, from a quarter to a half of it; in each group of 2 rows the first row is a single document. `query_route`: entries k * 16 to (k + 1) * 16 - 1 of a row are distinct positions from k * 128 to (k + 1) * 128 - 1. `kv_route`: entries k * 16 to (k + 1) * 16 - 1 of a row are distinct positions from k * 128 to (k + 1) * 128 - 1. `ffn_route`: entries k * 16 to (k + 1) * 16 - 1 of a row are distinct positions from k * 128 to (k + 1) * 128 - 1.
All inputs are finite; a program needn't handle non-finite values.
Results may differ from a plain program's by a relative error of at most 0.015.
Values may be sent and summed in bfloat16 or wider, within the bound.
No kernel may reach another device: no remote copies, remote signals or barrier semaphores. Data moves between devices by JAX's collectives and lax.ppermute only.
A program may use at most 256 MiB of HBM per device.

v0:
```python
import math

import jax
import jax.numpy as jnp
from jax import lax
from jax.sharding import PartitionSpec as P

DL = 96
DH = 64
RADIUS = 64


PRECISE = lax.Precision.HIGHEST
EPSILON = 1e-06
NEG_FILL = -1e30


def with_halo(value, sides, width):
    for axis, dim in sides:
        peers, length = (lax.axis_size(axis), value.shape[dim])
        up = [(i, (i + 1) % peers) for i in range(peers - 1)]
        down = [(j, i) for i, j in up]
        last = lax.slice_in_dim(value, length - width, length, axis=dim)
        leading = lax.slice_in_dim(value, 0, width, axis=dim)
        before = lax.ppermute(last, axis, up)
        after = lax.ppermute(leading, axis, down)
        value = jnp.concatenate([before, value, after], axis=dim)
    return value


def shifted(block, axis, distance):
    devices = range(lax.axis_size(axis))
    route = [(i - distance, i) for i in devices if i - distance in devices]
    return lax.ppermute(block, axis, route)


def rms_factor(hidden):
    return lax.rsqrt(jnp.mean(hidden * hidden, axis=-1, keepdims=True) + EPSILON)


def norm_back(hidden, factor, gain_vec, upstream):
    weighted = upstream * gain_vec
    inner_mean = jnp.mean(weighted * hidden, axis=-1, keepdims=True)
    input_grad = factor * weighted - hidden * (factor * factor * factor) * inner_mean
    gain_grad = jnp.sum(upstream * hidden * factor, axis=(0, 1))
    return (input_grad, gain_grad)


def pick_rows(source, positions):
    return jnp.take_along_axis(source, positions[..., None], axis=1)


def place_rows(values, positions, extent):
    onehot = (positions[..., None] == jnp.arange(extent)[None, None, :]).astype(jnp.float32)
    return jnp.einsum("rqs,rqd->rsd", onehot, values, precision=PRECISE)


def glu_value(gate_part, up_part):
    return jax.nn.gelu(gate_part, approximate=True) * up_part


def geglu_forward(inputs, weight, inner_width):
    both_parts = jnp.einsum("rsd,de->rse", inputs, weight, preferred_element_type=jnp.float32)
    gate_part = both_parts[..., :inner_width]
    up_part = both_parts[..., inner_width:]
    return (gate_part, up_part, glu_value(gate_part, up_part).astype(jnp.bfloat16))


def geglu_backward(inputs, weight, gate_part, up_part, hidden_low, down_weight, upstream_low):
    down_grad = jnp.einsum(
        "rsf,rsd->fd", hidden_low, upstream_low, preferred_element_type=jnp.float32
    )
    hidden_grad = jnp.einsum(
        "rsd,fd->rsf", upstream_low, down_weight, preferred_element_type=jnp.float32
    )
    _, pull_back = jax.vjp(glu_value, gate_part, up_part)
    gate_grad, up_grad = pull_back(hidden_grad)
    both_low = jnp.concatenate([gate_grad, up_grad], axis=-1).astype(jnp.bfloat16)
    weight_grad = jnp.einsum("rsd,rse->de", inputs, both_low, preferred_element_type=jnp.float32)
    input_grad = jnp.einsum("rse,de->rsd", both_low, weight, preferred_element_type=jnp.float32)
    return (weight_grad, down_grad, input_grad)


def local(
    tokens,
    segments,
    query_route,
    kv_route,
    ffn_route,
    grad_out,
    attn_gain,
    light_qkv,
    light_out,
    heavy_q,
    heavy_kv,
    heavy_out,
    route_query,
    ffn_gain,
    light_gate_up,
    light_down,
    heavy_gate_up,
    heavy_down,
    route_ffn,
):
    row_count, seg_span, model_width = tokens.shape
    heavy_width = heavy_q.shape[1]
    heavy_heads = heavy_width // DH
    light_heads = model_width // DL
    ffn_light = light_down.shape[0]
    ffn_heavy = heavy_down.shape[0]
    devices = lax.axis_size("seq")
    seq_place = lax.axis_index("seq")
    anchor = seq_place * seg_span
    routed_all = query_route.shape[1]
    routed_own = routed_all // devices
    own_start = seq_place * routed_own
    seg_all = lax.all_gather(segments, "seq", axis=1, tiled=True)
    hidden = tokens.astype(jnp.float32)
    factor_one = rms_factor(hidden)
    normed = hidden * factor_one * attn_gain
    normed_low = normed.astype(jnp.bfloat16)
    qkv_low = jnp.einsum(
        "rsd,de->rse", normed_low, light_qkv, preferred_element_type=jnp.float32
    ).astype(jnp.bfloat16)
    query_low = qkv_low[..., :model_width].reshape(row_count, seg_span, light_heads, DL)
    kv_rim = with_halo(qkv_low[..., model_width:], (("seq", 1),), RADIUS)
    extent = seg_span + 2 * RADIUS
    key_ext = kv_rim[..., :model_width].reshape(row_count, extent, light_heads, DL)
    val_ext = kv_rim[..., model_width:].reshape(row_count, extent, light_heads, DL)
    seg_pad = jnp.pad(seg_all, ((0, 0), (RADIUS, RADIUS)), constant_values=-2)
    key_seg = lax.dynamic_slice_in_dim(seg_pad, anchor, extent, 1)
    offset = jnp.arange(seg_span)[:, None] - jnp.arange(extent)[None, :] + RADIUS
    allowed = ((jnp.abs(offset) <= RADIUS)[None] & (segments[:, :, None] == key_seg[:, None, :]))[
        :, None
    ]
    light_scale = 1.0 / math.sqrt(DL)
    scores = (
        jnp.einsum("rqhd,rkhd->rhqk", query_low, key_ext, preferred_element_type=jnp.float32)
        * light_scale
    )
    scores = jnp.where(allowed, scores, NEG_FILL)
    numerators = jnp.exp(scores - jnp.max(scores, axis=-1, keepdims=True))
    probs_light = numerators / jnp.sum(numerators, axis=-1, keepdims=True)
    probs_low = probs_light.astype(jnp.bfloat16)
    light_mix = (
        jnp.einsum("rhqk,rkhd->rqhd", probs_low, val_ext, preferred_element_type=jnp.float32)
        .reshape(row_count, seg_span, model_width)
        .astype(jnp.bfloat16)
    )
    light_attn = jnp.einsum("rsi,id->rsd", light_mix, light_out, preferred_element_type=jnp.float32)
    own_query = lax.dynamic_slice_in_dim(query_route, own_start, routed_own, 1) - anchor
    own_key = lax.dynamic_slice_in_dim(kv_route, own_start, routed_own, 1) - anchor
    query_seg_all = jnp.take_along_axis(seg_all, query_route, axis=1)
    key_seg_all = jnp.take_along_axis(seg_all, kv_route, axis=1)
    query_seg_own = lax.dynamic_slice_in_dim(query_seg_all, own_start, routed_own, 1)
    query_rows = pick_rows(normed_low, own_query)
    key_rows = pick_rows(normed_low, own_key)
    heavy_query = jnp.einsum(
        "rqd,de->rqe", query_rows, heavy_q, preferred_element_type=jnp.float32
    ).astype(jnp.bfloat16)
    heavy_keyval = jnp.einsum(
        "rqd,de->rqe", key_rows, heavy_kv, preferred_element_type=jnp.float32
    ).astype(jnp.bfloat16)
    keyval_all = lax.all_gather(heavy_keyval, "seq", axis=1, tiled=True)
    query_heads = heavy_query.reshape(row_count, routed_own, heavy_heads, DH)
    keys_all = keyval_all[..., :heavy_width].reshape(row_count, routed_all, heavy_heads, DH)
    vals_all = keyval_all[..., heavy_width:].reshape(row_count, routed_all, heavy_heads, DH)
    heavy_scale = 1.0 / math.sqrt(DH)
    routed_raw = (
        jnp.einsum("rqhd,rkhd->rhqk", query_heads, keys_all, preferred_element_type=jnp.float32)
        * heavy_scale
    )
    routed_allowed = (query_seg_own[:, :, None] == key_seg_all[:, None, :])[:, None]
    routed_masked = jnp.where(routed_allowed, routed_raw, NEG_FILL)
    peak_score = jnp.maximum(jnp.max(routed_masked, axis=-1, keepdims=True), 0.0)
    routed_num = jnp.exp(routed_masked - peak_score)
    denominator = jnp.exp(-peak_score) + jnp.sum(routed_num, axis=-1, keepdims=True)
    probs_heavy = routed_num / denominator
    heavy_low = probs_heavy.astype(jnp.bfloat16)
    heavy_mix = (
        jnp.einsum("rhqk,rkhd->rqhd", heavy_low, vals_all, preferred_element_type=jnp.float32)
        .reshape(row_count, routed_own, heavy_width)
        .astype(jnp.bfloat16)
    )
    heavy_proj = jnp.einsum("rqi,id->rqd", heavy_mix, heavy_out, preferred_element_type=jnp.float32)
    query_normed = pick_rows(normed, own_query)
    route_query_full = route_query.astype(jnp.float32)
    query_gate = jax.nn.sigmoid(
        jnp.einsum("rqd,d->rq", query_normed, route_query_full, precision=PRECISE)
    )
    heavy_attn = place_rows(query_gate[..., None] * heavy_proj, own_query, seg_span)
    middle = hidden + light_attn + heavy_attn
    factor_two = rms_factor(middle)
    normed_two = middle * factor_two * ffn_gain
    low_two = normed_two.astype(jnp.bfloat16)
    gate_light, up_light, hidden_light = geglu_forward(low_two, light_gate_up, ffn_light)
    light_ff = jnp.einsum(
        "rsf,fd->rsd", hidden_light, light_down, preferred_element_type=jnp.float32
    )
    own_ffn = ffn_route - anchor
    ffn_rows = pick_rows(low_two, own_ffn)
    gate_heavy, up_heavy, hidden_heavy = geglu_forward(ffn_rows, heavy_gate_up, ffn_heavy)
    heavy_ffn_proj = jnp.einsum(
        "rqf,fd->rqd", hidden_heavy, heavy_down, preferred_element_type=jnp.float32
    )
    ffn_normed = pick_rows(normed_two, own_ffn)
    route_ffn_full = route_ffn.astype(jnp.float32)
    ffn_gate = jax.nn.sigmoid(
        jnp.einsum("rqd,d->rq", ffn_normed, route_ffn_full, precision=PRECISE)
    )
    heavy_ff = place_rows(ffn_gate[..., None] * heavy_ffn_proj, own_ffn, seg_span)
    outputs = (middle + light_ff + heavy_ff).astype(jnp.bfloat16)
    valid_rows = (segments >= 0).astype(jnp.float32)[..., None]
    squares = jnp.stack(
        [
            jnp.sum(valid_rows * branch * branch)
            for branch in (hidden, light_attn, heavy_attn, light_ff, heavy_ff)
        ]
    )
    squares_all, valid_all = lax.psum((squares, jnp.sum(valid_rows)), ("dp", "seq"))
    rms_stats = jnp.sqrt(squares_all / (valid_all * model_width))
    upstream = grad_out.astype(jnp.float32)
    light_gate_up_grad, light_down_grad, normed_two_grad = geglu_backward(
        low_two, light_gate_up, gate_light, up_light, hidden_light, light_down, grad_out
    )
    ffn_upstream = pick_rows(upstream, own_ffn)
    ffn_gate_grad = jnp.sum(ffn_upstream * heavy_ffn_proj, axis=-1)
    ffn_low = (ffn_upstream * ffn_gate[..., None]).astype(jnp.bfloat16)
    heavy_gate_up_grad, heavy_down_grad, ffn_rows_grad = geglu_backward(
        ffn_rows, heavy_gate_up, gate_heavy, up_heavy, hidden_heavy, heavy_down, ffn_low
    )
    ffn_logit_grad = ffn_gate_grad * ffn_gate * (1.0 - ffn_gate)
    route_ffn_grad = jnp.einsum("rq,rqd->d", ffn_logit_grad, ffn_normed, precision=PRECISE)
    ffn_rows_grad = ffn_rows_grad + ffn_logit_grad[..., None] * route_ffn_full
    normed_two_grad = normed_two_grad + place_rows(ffn_rows_grad, own_ffn, seg_span)
    middle_norm_grad, ffn_gain_grad = norm_back(middle, factor_two, ffn_gain, normed_two_grad)
    middle_grad = upstream + middle_norm_grad
    middle_low = middle_grad.astype(jnp.bfloat16)
    light_out_grad = jnp.einsum(
        "rsi,rsd->id", light_mix, middle_low, preferred_element_type=jnp.float32
    )
    mix_grad = (
        jnp.einsum("rsd,id->rsi", middle_low, light_out, preferred_element_type=jnp.float32)
        .astype(jnp.bfloat16)
        .reshape(row_count, seg_span, light_heads, DL)
    )
    val_grad = jnp.einsum(
        "rhqk,rqhd->rkhd", probs_low, mix_grad, preferred_element_type=jnp.float32
    )
    prob_grad = jnp.einsum("rqhd,rkhd->rhqk", mix_grad, val_ext, preferred_element_type=jnp.float32)
    score_grad = (
        probs_light * (prob_grad - jnp.sum(probs_light * prob_grad, axis=-1, keepdims=True))
    ).astype(jnp.bfloat16)
    query_grad = (
        jnp.einsum("rhqk,rkhd->rqhd", score_grad, key_ext, preferred_element_type=jnp.float32)
        * light_scale
    )
    key_grad = (
        jnp.einsum("rhqk,rqhd->rkhd", score_grad, query_low, preferred_element_type=jnp.float32)
        * light_scale
    )
    rim_grad = jnp.concatenate(
        [
            key_grad.reshape(row_count, extent, model_width),
            val_grad.reshape(row_count, extent, model_width),
        ],
        axis=-1,
    )
    from_right = shifted(rim_grad[:, :RADIUS].astype(jnp.bfloat16), "seq", -1).astype(jnp.float32)
    from_left = shifted(rim_grad[:, seg_span + RADIUS :].astype(jnp.bfloat16), "seq", 1).astype(
        jnp.float32
    )
    inner_grad = rim_grad[:, RADIUS : seg_span + RADIUS]
    inner_grad = (
        inner_grad
        + jnp.pad(from_left, ((0, 0), (0, seg_span - RADIUS), (0, 0)))
        + jnp.pad(from_right, ((0, 0), (seg_span - RADIUS, 0), (0, 0)))
    )
    qkv_grad_low = jnp.concatenate(
        [query_grad.reshape(row_count, seg_span, model_width), inner_grad], axis=-1
    ).astype(jnp.bfloat16)
    light_qkv_grad = jnp.einsum(
        "rsd,rse->de", normed_low, qkv_grad_low, preferred_element_type=jnp.float32
    )
    normed_grad = jnp.einsum(
        "rse,de->rsd", qkv_grad_low, light_qkv, preferred_element_type=jnp.float32
    )
    heavy_upstream = pick_rows(middle_grad, own_query)
    query_gate_grad = jnp.sum(heavy_upstream * heavy_proj, axis=-1)
    proj_low = (heavy_upstream * query_gate[..., None]).astype(jnp.bfloat16)
    heavy_out_grad = jnp.einsum(
        "rqi,rqd->id", heavy_mix, proj_low, preferred_element_type=jnp.float32
    )
    heavy_mix_grad = (
        jnp.einsum("rqd,id->rqi", proj_low, heavy_out, preferred_element_type=jnp.float32)
        .astype(jnp.bfloat16)
        .reshape(row_count, routed_own, heavy_heads, DH)
    )
    routed_prob_grad = jnp.einsum(
        "rqhd,rkhd->rhqk", heavy_mix_grad, vals_all, preferred_element_type=jnp.float32
    )
    routed_delta = jnp.sum(probs_heavy * routed_prob_grad, axis=-1, keepdims=True)
    routed_score_grad = (probs_heavy * (routed_prob_grad - routed_delta)).astype(jnp.bfloat16)
    heavy_query_grad = (
        (
            jnp.einsum(
                "rhqk,rkhd->rqhd", routed_score_grad, keys_all, preferred_element_type=jnp.float32
            )
            * heavy_scale
        )
        .reshape(row_count, routed_own, heavy_width)
        .astype(jnp.bfloat16)
    )
    key_term = (
        jnp.einsum(
            "rhqk,rqhd->rkhd", routed_score_grad, query_heads, preferred_element_type=jnp.float32
        )
        * heavy_scale
    )
    val_term = jnp.einsum(
        "rhqk,rqhd->rkhd", heavy_low, heavy_mix_grad, preferred_element_type=jnp.float32
    )
    keyval_term = jnp.concatenate(
        [
            key_term.reshape(row_count, routed_all, heavy_width),
            val_term.reshape(row_count, routed_all, heavy_width),
        ],
        axis=-1,
    )
    keyval_grad = lax.psum_scatter(keyval_term, "seq", scatter_dimension=1, tiled=True)
    keyval_low = keyval_grad.astype(jnp.bfloat16)
    heavy_q_grad = jnp.einsum(
        "rqd,rqe->de", query_rows, heavy_query_grad, preferred_element_type=jnp.float32
    )
    heavy_kv_grad = jnp.einsum(
        "rqd,rqe->de", key_rows, keyval_low, preferred_element_type=jnp.float32
    )
    query_logit_grad = query_gate_grad * query_gate * (1.0 - query_gate)
    route_query_grad = jnp.einsum("rq,rqd->d", query_logit_grad, query_normed, precision=PRECISE)
    query_rows_grad = (
        jnp.einsum("rqe,de->rqd", heavy_query_grad, heavy_q, preferred_element_type=jnp.float32)
        + query_logit_grad[..., None] * route_query_full
    )
    key_rows_grad = jnp.einsum(
        "rqe,de->rqd", keyval_low, heavy_kv, preferred_element_type=jnp.float32
    )
    normed_grad = (
        normed_grad
        + place_rows(query_rows_grad, own_query, seg_span)
        + place_rows(key_rows_grad, own_key, seg_span)
    )
    hidden_norm_grad, attn_gain_grad = norm_back(hidden, factor_one, attn_gain, normed_grad)
    grad_tokens = (middle_grad + hidden_norm_grad).astype(jnp.bfloat16)
    grad_terms = (
        attn_gain_grad,
        light_qkv_grad,
        light_out_grad,
        heavy_q_grad,
        heavy_kv_grad,
        heavy_out_grad,
        route_query_grad,
        ffn_gain_grad,
        light_gate_up_grad,
        light_down_grad,
        heavy_gate_up_grad,
        heavy_down_grad,
        route_ffn_grad,
    )
    shares = (
        lax.psum_scatter(grad_terms[0], "seq", scatter_dimension=0, tiled=True),
        lax.psum_scatter(grad_terms[1], "seq", scatter_dimension=0, tiled=True),
        lax.psum_scatter(grad_terms[2], "seq", scatter_dimension=0, tiled=True),
        lax.psum_scatter(grad_terms[3], "seq", scatter_dimension=0, tiled=True),
        lax.psum_scatter(grad_terms[4], "seq", scatter_dimension=0, tiled=True),
        lax.psum_scatter(grad_terms[5], "seq", scatter_dimension=0, tiled=True),
        lax.psum_scatter(grad_terms[6], "seq", scatter_dimension=0, tiled=True),
        lax.psum_scatter(grad_terms[7], "seq", scatter_dimension=0, tiled=True),
        lax.psum_scatter(grad_terms[8], "seq", scatter_dimension=0, tiled=True),
        lax.psum_scatter(grad_terms[9], "seq", scatter_dimension=0, tiled=True),
        lax.psum_scatter(grad_terms[10], "seq", scatter_dimension=0, tiled=True),
        lax.psum_scatter(grad_terms[11], "seq", scatter_dimension=0, tiled=True),
        lax.psum_scatter(grad_terms[12], "seq", scatter_dimension=0, tiled=True),
    )
    matrix_sum = (
        lax.psum_scatter(
            shares[1].astype(jnp.bfloat16), "dp", scatter_dimension=1, tiled=True
        ).astype(jnp.float32),
        lax.psum_scatter(
            shares[2].astype(jnp.bfloat16), "dp", scatter_dimension=1, tiled=True
        ).astype(jnp.float32),
        lax.psum_scatter(
            shares[3].astype(jnp.bfloat16), "dp", scatter_dimension=1, tiled=True
        ).astype(jnp.float32),
        lax.psum_scatter(
            shares[4].astype(jnp.bfloat16), "dp", scatter_dimension=1, tiled=True
        ).astype(jnp.float32),
        lax.psum_scatter(
            shares[5].astype(jnp.bfloat16), "dp", scatter_dimension=1, tiled=True
        ).astype(jnp.float32),
        lax.psum_scatter(
            shares[8].astype(jnp.bfloat16), "dp", scatter_dimension=1, tiled=True
        ).astype(jnp.float32),
        lax.psum_scatter(
            shares[9].astype(jnp.bfloat16), "dp", scatter_dimension=1, tiled=True
        ).astype(jnp.float32),
        lax.psum_scatter(
            shares[10].astype(jnp.bfloat16), "dp", scatter_dimension=1, tiled=True
        ).astype(jnp.float32),
        lax.psum_scatter(
            shares[11].astype(jnp.bfloat16), "dp", scatter_dimension=1, tiled=True
        ).astype(jnp.float32),
    )
    vector_sum = lax.psum((shares[0], shares[6], shares[7], shares[12]), "dp")
    return (
        outputs,
        grad_tokens,
        vector_sum[0],
        matrix_sum[0],
        matrix_sum[1],
        matrix_sum[2],
        matrix_sum[3],
        matrix_sum[4],
        vector_sum[1],
        vector_sum[2],
        matrix_sum[5],
        matrix_sum[6],
        matrix_sum[7],
        matrix_sum[8],
        vector_sum[3],
        rms_stats,
    )


def solution(mesh):
    placed = (
        P("dp", "seq", None),
        P("dp", "seq"),
        P("dp", None),
        P("dp", None),
        P("dp", "seq"),
        P("dp", "seq", None),
        P(),
        P(),
        P(),
        P(),
        P(),
        P(),
        P(),
        P(),
        P(),
        P(),
        P(),
        P(),
        P(),
    )
    return jax.shard_map(
        local,
        mesh=mesh,
        in_specs=placed,
        out_specs=(
            P("dp", "seq", None),
            P("dp", "seq", None),
            P("seq"),
            P("seq", "dp"),
            P("seq", "dp"),
            P("seq", "dp"),
            P("seq", "dp"),
            P("seq", "dp"),
            P("seq"),
            P("seq"),
            P("seq", "dp"),
            P("seq", "dp"),
            P("seq", "dp"),
            P("seq", "dp"),
            P("seq"),
            P(),
        ),
        check_vma=False,
    )
```

profile of v0, /device:TPU:0, one launch (start us, length us, event | category | flops | bytes accessed | tf_op | source)
XLA Modules:
  0.0 1377.8 jit_solution(18068979061425199381)
XLA Ops:
  26.0 23.3 %all_gather.6 = s32[2,2048]{1,0:T(2,128)S(1)} all-gather(s32[2,128]{1,0:T(2,128)} %param.26), channel_id=1, replica_groups=mesh['dp'=2,'seq'=16] {'seq'}, dimensions={1}, use_global_device_ids=true | all-gather | bytes 17408 | tf_op jit(solution)/shard_map/all_gather | solution.py:117
  57.4 7.2 gather_fusion.2
  77.0 7.3 gather_fusion.3
  151.1 6.9 fusion.3
  167.6 5.5 fusion.95
  228.0 5.0 convolution_bitcast_fusion.3
  271.8 4.8 reduce-scatter.32.cloned.1.call-done
  281.2 7.4 convolution_bitcast_fusion.1
  288.7 13.4 convolution_bitcast_fusion
  302.2 40.2 %reduce-scatter.36.cloned.1.call-done = f32[48,768]{1,0:T(8,128)} async-done(((f32[768,768]{1,0:T(8,128)}), f32[48,768]{1,0:T(8,128)}) %reduce-scatter.36.cloned.1.call-update) | async-done | bytes 147472 | tf_op jit(solution)/shard_map/reduce_scatter | solution.py:372
  345.9 62.6 %reduce-scatter.38.cloned.1.call-done = f32[48,768]{1,0:T(8,128)} async-done(((f32[768,768]{1,0:T(8,128)}), f32[48,768]{1,0:T(8,128)}) %reduce-scatter.38.cloned.1.call-update) | async-done | bytes 147472 | tf_op jit(solution)/shard_map/reduce_scatter | solution.py:373
  411.8 62.3 %reduce-scatter.44.cloned.1.call-done = f32[48,768]{1,0:T(8,128)} async-done(((f32[768,768]{1,0:T(8,128)}), f32[48,768]{1,0:T(8,128)}) %reduce-scatter.44.cloned.1.call-update) | async-done | bytes 147472 | tf_op jit(solution)/shard_map/reduce_scatter | solution.py:375
  477.5 66.2 %reduce-scatter.50.cloned.1.call-done = f32[64,768]{1,0:T(8,128)} async-done(((f32[1024,768]{1,0:T(8,128)}), f32[64,768]{1,0:T(8,128)}) %reduce-scatter.50.cloned.1.call-update) | async-done | bytes 196624 | tf_op jit(solution)/shard_map/reduce_scatter | solution.py:379
  547.0 85.3 %reduce-scatter.46.cloned.1.call-done = f32[48,2048]{1,0:T(8,128)} async-done(((f32[768,2048]{1,0:T(8,128)}), f32[48,2048]{1,0:T(8,128)}) %reduce-scatter.46.cloned.1.call-update) | async-done | bytes 393232 | tf_op jit(solution)/shard_map/reduce_scatter | solution.py:378
  634.1 91.6 %reduce-scatter.34.cloned.1.call-done = f32[48,2304]{1,0:T(8,128)} async-done(((f32[768,2304]{1,0:T(8,128)}), f32[48,2304]{1,0:T(8,128)}) %reduce-scatter.34.cloned.1.call-update) | async-done | bytes 442384 | tf_op jit(solution)/shard_map/reduce_scatter | solution.py:371
  729.5 75.6 %reduce-scatter.40.cloned.1.call-done = f32[48,1536]{1,0:T(8,128)} async-done(((f32[768,1536]{1,0:T(8,128)}), f32[48,1536]{1,0:T(8,128)}) %reduce-scatter.40.cloned.1.call-update) | async-done | bytes 294928 | tf_op jit(solution)/shard_map/reduce_scatter | solution.py:374
  811.1 131.6 %reduce-scatter.56.cloned.1.call-done = f32[256,768]{1,0:T(8,128)} async-done(((f32[4096,768]{1,0:T(8,128)}), f32[256,768]{1,0:T(8,128)}) %reduce-scatter.56.cloned.1.call-update) | async-done | bytes 786448 | tf_op jit(solution)/shard_map/reduce_scatter | solution.py:381
  954.4 235.6 %reduce-scatter.52.cloned.1.call-done = f32[48,8192]{1,0:T(8,128)} async-done(((f32[768,8192]{1,0:T(8,128)}), f32[48,8192]{1,0:T(8,128)}) %reduce-scatter.52.cloned.1.call-update) | async-done | bytes 1572880 | tf_op jit(solution)/shard_map/reduce_scatter | solution.py:380
  1195.9 6.8 reduce-scatter.60.cloned.1.call-done
  1205.7 10.8 reduce-scatter.62.cloned.1.call-done
  1219.5 10.1 reduce-scatter.64.cloned.1.call-done
  1241.9 39.6 %all-reduce.7 = (f32[5]{0:T(128)}, f32[]{:T(128)}) all-reduce(f32[5]{0:T(128)} %stack.23, f32[]{:T(128)} %fusion.174), channel_id=1, replica_groups=mesh['dp'=2,'seq'=16] {'dp','seq'}, use_global_device_ids=true, to_apply=%region_46.50 | all-reduce | flops 6 | bytes 48 | tf_op jit(solution)/shard_map/psum | solution.py:220
  1281.5 60.3 %all-reduce.8 = (f32[768]{0:T(1024)}, f32[768]{0:T(1024)}, f32[768]{0:T(1024)}, f32[768]{0:T(1024)}) all-reduce(f32[768]{0:T(1024)} %get-tuple-element.21, f32[768]{0:T(1024)S(1)} %convolution_reduce_fusion.1, f32[768]{0:T(1024)S(1)} %copy-done.52, f32[768]{0:T(1024)S(1)} %copy-done.53), channel_id=3, replica_groups=mesh['dp'=2,'seq'=16] {'seq'}, use_global_device_ids=true, to_apply=%region_14.18.clone | all-reduce | flops 3072 | bytes 24576
  1346.0 5.6 all-reduce.9
  (372 shorter events, 296.3 us)
Async XLA Ops:
  7.2 114.1 %all-gather.2.cloned.1.call-start = ((), (), s32[]{:S(2)}) async-start(), calls=%async_computation.19 | async-start | bytes 1671168 | tf_op jit(solution)/shard_map/all_gather | solution.py:164
  13.6 92.4 %collective-permute-start.1 = (bf16[2,64,1536]{2,1,0:T(8,128)(2,1)}, bf16[2,64,1536]{2,1,0:T(8,128)(2,1)}, u32[]{:S(2)}, u32[]{:S(2)}) collective-permute-start(bf16[2,64,1536]{2,1,0:T(8,128)(2,1)} %get-tuple-element.63), channel_id=1, source_target_pairs={{1,0},{2,1},{3,2},{4,3},{5,4},{6,5},{7,6},{8,7},{9,8},{10,9},{11,1... | collective-permute-start | bytes 1179656 | tf_op jit(solution)/shard_map/ppermute | solution.py:26
  14.9 91.1 %collective-permute-start = (bf16[2,64,1536]{2,1,0:T(8,128)(2,1)}, bf16[2,64,1536]{2,1,0:T(8,128)(2,1)}, u32[]{:S(2)}, u32[]{:S(2)}) collective-permute-start(bf16[2,64,1536]{2,1,0:T(8,128)(2,1)} %get-tuple-element.62), channel_id=1, source_target_pairs={{0,1},{1,2},{2,3},{3,4},{4,5},{5,6},{6,7},{7,8},{8,9},{9,10},{10,1... | collective-permute-start | bytes 1179656 | tf_op jit(solution)/shard_map/ppermute | solution.py:25
  25.3 251.3 %reduce-scatter.32.cloned.1.call-start = ((), (), s32[]{:S(2)}) async-start(), calls=%async_computation.20 | async-start | bytes 3342336 | tf_op jit(solution)/shard_map/reduce_scatter | solution.py:330
  211.0 131.4 %reduce-scatter.36.cloned.1.call-start = ((), (), s32[]{:S(2)}) async-start(), calls=%async_computation.22 | async-start | bytes 2506752 | tf_op jit(solution)/shard_map/reduce_scatter | solution.py:372
  214.3 194.2 %reduce-scatter.38.cloned.1.call-start = ((), (), s32[]{:S(2)}) async-start(), calls=%async_computation.23 | async-start | bytes 2506752 | tf_op jit(solution)/shard_map/reduce_scatter | solution.py:373
  221.1 253.1 %reduce-scatter.44.cloned.1.call-start = ((), (), s32[]{:S(2)}) async-start(), calls=%async_computation.26 | async-start | bytes 2506752 | tf_op jit(solution)/shard_map/reduce_scatter | solution.py:375
  224.0 319.6 %reduce-scatter.50.cloned.1.call-start = ((), (), s32[]{:S(2)}) async-start(), calls=%async_computation.29 | async-start | bytes 3342336 | tf_op jit(solution)/shard_map/reduce_scatter | solution.py:379
  227.6 404.7 %reduce-scatter.46.cloned.1.call-start = ((), (), s32[]{:S(2)}) async-start(), calls=%async_computation.27 | async-start | bytes 6684672 | tf_op jit(solution)/shard_map/reduce_scatter | solution.py:378
  233.1 492.6 %reduce-scatter.34.cloned.1.call-start = ((), (), s32[]{:S(2)}) async-start(), calls=%async_computation.21 | async-start | bytes 7520256 | tf_op jit(solution)/shard_map/reduce_scatter | solution.py:371
  256.7 8.2 collective-permute-start.3
  258.0 6.9 collective-permute-start.2
  271.7 533.4 %reduce-scatter.40.cloned.1.call-start = ((), (), s32[]{:S(2)}) async-start(), calls=%async_computation.24 | async-start | bytes 5013504 | tf_op jit(solution)/shard_map/reduce_scatter | solution.py:374
  280.6 662.1 %reduce-scatter.56.cloned.1.call-start = ((), (), s32[]{:S(2)}) async-start(), calls=%async_computation.32 | async-start | bytes 13369344 | tf_op jit(solution)/shard_map/reduce_scatter | solution.py:381
  288.7 901.3 %reduce-scatter.52.cloned.1.call-start = ((), (), s32[]{:S(2)}) async-start(), calls=%async_computation.30 | async-start | bytes 26738688 | tf_op jit(solution)/shard_map/reduce_scatter | solution.py:380
  302.1 900.6 %reduce-scatter.60.cloned.1.call-start = ((), (), s32[]{:S(2)}) async-start(), calls=%async_computation.34 | async-start | bytes 294912
  345.7 870.8 %reduce-scatter.62.cloned.1.call-start = ((), (), s32[]{:S(2)}) async-start(), calls=%async_computation.35 | async-start | bytes 294912
  411.7 817.8 %reduce-scatter.64.cloned.1.call-start = ((), (), s32[]{:S(2)}) async-start(), calls=%async_computation.36 | async-start | bytes 294912
  477.4 878.4 %reduce-scatter.66.cloned.1.call-start = ((), (), s32[]{:S(2)}) async-start(), calls=%async_computation.37 | async-start | bytes 294912
  546.9 811.9 %reduce-scatter.48.cloned.1.call-start = ((), (), s32[]{:S(2)}) async-start(), calls=%async_computation.28 | async-start | bytes 294912 | tf_op jit(solution)/shard_map/reduce_scatter | solution.py:400
  634.0 726.4 %reduce-scatter.58.cloned.1.call-start = ((), (), s32[]{:S(2)}) async-start(), calls=%async_computation.33 | async-start | bytes 884736
  729.4 634.4 %reduce-scatter.42.cloned.1.call-start = ((), (), s32[]{:S(2)}) async-start(), calls=%async_computation.25 | async-start | bytes 221184 | tf_op jit(solution)/shard_map/reduce_scatter | solution.py:394
  806.8 558.6 %reduce-scatter.68.cloned.1.call-start = ((), (), s32[]{:S(2)}) async-start(), calls=%async_computation.38 | async-start | bytes 589824
  946.6 422.2 %reduce-scatter.54.cloned.1.call-start = ((), (), s32[]{:S(2)}) async-start(), calls=%async_computation.31 | async-start | bytes 1179648 | tf_op jit(solution)/shard_map/reduce_scatter | solution.py:406
  (78 other events, 784.3 us)
Sparse Core Ops, SparseCore 0:
  25.4 42.4 all-gather.1
  211.2 65.3 reduce-scatter.31
  280.4 61.9 reduce-scatter.35
  346.5 61.9 reduce-scatter.37
  412.1 62.0 reduce-scatter.43
  478.3 65.3 reduce-scatter.49
  548.1 84.1 reduce-scatter.45
  636.3 89.3 reduce-scatter.33
  730.0 75.0 reduce-scatter.39
  809.0 133.6 reduce-scatter.55
  946.8 243.1 reduce-scatter.51
  1192.6 10.0 reduce-scatter.59
  1205.5 10.9 reduce-scatter.61
  1218.6 10.9 reduce-scatter.63
  1231.6 10.9 reduce-scatter.65
  1244.7 10.9 reduce-scatter.47
  1257.8 15.4 reduce-scatter.57
  1276.0 10.4 reduce-scatter.41
  1288.8 13.0 reduce-scatter.67
  1304.0 17.4 reduce-scatter.53
where the time goes:
time: 1390 us; the launch traced here: 1380 us
  waiting for transfers between devices  884 us (64%)
  matrix products  144 us (10%)
  blocking collectives  129 us (9%)
  local copies, waits for them, and re-layouts  122 us (9%)
  other arithmetic  70.6 us (5%)
  between operations  16.6 us (1%)
    reduce_scatter x1, waiting for transfers between devices, local(): lax.psum_scatter(grad_terms[10], 'seq', scatter_dimension=0, tiled=True)  236 us
    reduce_scatter x1, waiting for transfers between devices, local(): lax.psum_scatter(grad_terms[11], 'seq', scatter_dimension=0, tiled=True)  132 us
    reduce_scatter x1, waiting for transfers between devices, local(): lax.psum_scatter(grad_terms[1], 'seq', scatter_dimension=0, tiled=True)  91.6 us
    reduce_scatter x1, waiting for transfers between devices, local(): lax.psum_scatter(grad_terms[8], 'seq', scatter_dimension=0, tiled=True)  85.3 us
    reduce_scatter x1, waiting for transfers between devices, local(): lax.psum_scatter(grad_terms[4], 'seq', scatter_dimension=0, tiled=True)  75.6 us
    reduce_scatter x1, waiting for transfers between devices, local(): lax.psum_scatter(grad_terms[9], 'seq', scatter_dimension=0, tiled=True)  66.2 us
    reduce_scatter x1, waiting for transfers between devices, local(): lax.psum_scatter(grad_terms[3], 'seq', scatter_dimension=0, tiled=True)  62.6 us
    reduce_scatter x1, waiting for transfers between devices, local(): lax.psum_scatter(grad_terms[5], 'seq', scatter_dimension=0, tiled=True)  62.3 us
  transfers between devices with their start and end apart: 24, of which 13 were waited for; matrix products, arithmetic and copies ran while one was open for 17% of the time, Pallas kernels for 0%

commit v1 on v0

v1 whole, which is shorter than its diff:
```python
import math

import jax
import jax.numpy as jnp
from jax import lax
from jax.sharding import PartitionSpec as P

DL = 96
DH = 64
RADIUS = 64
LANES = 128


PRECISE = lax.Precision.HIGHEST
EPSILON = 1e-06
NEG_FILL = -1e30
F32 = jnp.float32
BF16 = jnp.bfloat16


def swap(value, axis, bit):
    return lax.ppermute(value, axis, [(i, i ^ bit) for i in range(lax.axis_size(axis))])


def shifted(block, axis, distance):
    devices = range(lax.axis_size(axis))
    route = [(i - distance, i) for i in devices if i - distance in devices]
    return lax.ppermute(block, axis, route)


def gather_blocks(block):
    held = block[None]
    bit = lax.axis_size("seq") // 2
    while bit:
        held = jnp.concatenate([held, swap(held, "seq", bit)], axis=0)
        bit //= 2
    return held


def add_halves(value, dim, axis, bit, out_type=BF16):
    half = value.shape[dim] // 2
    keep = lax.slice_in_dim(value, 0, half, axis=dim)
    sent = lax.slice_in_dim(value, half, 2 * half, axis=dim)
    return (keep.astype(F32) + swap(sent, axis, bit).astype(F32)).astype(out_type)


def scatter_sum(slots):
    devices = lax.axis_size("seq")
    rows = slots.shape[2]
    slots = add_halves(slots, 0, "seq", 1)
    left, right = slots[:, :, : rows // 2], slots[:, :, rows // 2 :]
    left = add_halves(left, 0, "seq", 2)
    right = add_halves(right, 1, "dp", 1)
    left = add_halves(left, 1, "dp", 1)
    right = add_halves(right, 0, "seq", 2)
    both = jnp.concatenate([left, right], axis=2)
    bit = 4
    while bit < devices:
        both = add_halves(both, 0, "seq", bit, BF16 if 2 * bit < devices else F32)
        bit *= 2
    return both[0, 0]


def slot_places(me, devices):
    bits = devices.bit_length() - 1
    places = [int(format(p, f"0{bits}b")[::-1], 2) for p in range(devices)]
    return jnp.array(places, jnp.int32) ^ me


def slot_columns(value, me, devices):
    width = value.shape[-1]
    block = width // devices
    order = (slot_places(me, devices)[:, None] * block + jnp.arange(block)[None, :]).reshape(-1)
    onehot = (jnp.arange(width)[:, None] == order[None, :]).astype(BF16)
    return jnp.dot(value, onehot, preferred_element_type=F32).astype(BF16)


def own_half_first(value, place):
    half = value.shape[-1] // 2
    first, second = value[..., :half], value[..., half:]
    return (jnp.where(place == 0, first, second), jnp.where(place == 0, second, first))


def slot_block(grad_halves, devices):
    stacked = jnp.stack(grad_halves)
    _, total, cols = stacked.shape
    parts = stacked.reshape(2, devices, total // devices, cols // LANES, LANES)
    return parts.transpose(1, 0, 3, 2, 4).reshape(devices, 2, -1, LANES).astype(BF16)


def unslot(rows, cols):
    return rows.reshape(cols // LANES, -1, LANES).transpose(1, 0, 2).reshape(-1, cols)


def slot_vectors(vectors, me, devices):
    block = vectors[0].shape[0] // devices
    table = jnp.stack(vectors, axis=-1).reshape(devices, block, len(vectors))
    table = jnp.take(table, slot_places(me, devices), axis=0)
    table = jnp.pad(table, ((0, 0), (0, 0), (0, LANES - len(vectors))))
    return jnp.broadcast_to(table[:, None], (devices, 2, block, LANES)).astype(BF16)


def split_parts(value):
    high = lax.reduce_precision(value, 8, 7)
    middle = lax.reduce_precision(value - high, 8, 7)
    return (high, middle, value - high - middle)


def rms_factor(hidden):
    return lax.rsqrt(jnp.mean(hidden * hidden, axis=-1, keepdims=True) + EPSILON)


def norm_back(hidden, factor, gain_vec, upstream):
    weighted = upstream * gain_vec
    inner_mean = jnp.mean(weighted * hidden, axis=-1, keepdims=True)
    return factor * weighted - hidden * (factor * factor * factor) * inner_mean


def pick_rows(source, positions):
    return jnp.take_along_axis(source, positions[..., None], axis=1)


def place_rows(values, positions, extent):
    onehot = (positions[..., None] == jnp.arange(extent)[None, None, :]).astype(F32)
    return jnp.einsum("rqs,rqd->rsd", onehot, values, precision=PRECISE)


def matmul(left, right):
    return jnp.einsum("...d,de->...e", left, right, preferred_element_type=F32)


def matmul_t(left, right):
    return jnp.einsum("...e,de->...d", left, right, preferred_element_type=F32)


def outer(left, right):
    return jnp.einsum("rsd,rse->de", left, right, preferred_element_type=F32)


def glu_value(gate_part, up_part):
    return jax.nn.gelu(gate_part, approximate=True) * up_part


def geglu(inputs, gate_up, down, upstream_low):
    width = down.shape[0]
    both = matmul(inputs, gate_up)
    gate_part, up_part = both[..., :width], both[..., width:]
    hidden, pull_back = jax.vjp(glu_value, gate_part, up_part)
    gate_grad, up_grad = pull_back(matmul_t(upstream_low, down))
    return (hidden.astype(BF16), gate_grad.astype(BF16), up_grad.astype(BF16))


def routed_probs(query_heads, key_heads, query_seg, key_seg):
    scores = jnp.einsum("rqd,rkd->rqk", query_heads, key_heads, preferred_element_type=F32)
    scores = scores / math.sqrt(DH)
    allowed = query_seg[:, :, None] == key_seg[:, None, :]
    scores = jnp.where(allowed, scores, NEG_FILL)
    peak = jnp.maximum(jnp.max(scores, axis=-1, keepdims=True), 0.0)
    numer = jnp.exp(scores - peak)
    return numer / (jnp.exp(-peak) + jnp.sum(numer, axis=-1, keepdims=True))


def heavy_forward(query, keys, vals, query_seg, key_seg):
    def head(parts):
        query_h, key_h, val_h = parts
        probs = routed_probs(query_h, key_h, query_seg, key_seg).astype(BF16)
        return jnp.einsum("rqk,rkd->rqd", probs, val_h, preferred_element_type=F32).astype(BF16)

    return join_heads(jax.vmap(head)((split_heads(query), split_heads(keys), split_heads(vals))))


def heavy_both(query, keys, vals, query_seg, key_seg, mix_grad):
    def head(parts, query_seg=query_seg, key_seg=key_seg):
        query_h, key_h, val_h, grad_h = parts
        probs = routed_probs(query_h, key_h, query_seg, key_seg)
        probs_low = probs.astype(BF16)
        mix = jnp.einsum("rqk,rkd->rqd", probs_low, val_h, preferred_element_type=F32)
        prob_grad = jnp.einsum("rqd,rkd->rqk", grad_h, val_h, preferred_element_type=F32)
        delta = jnp.sum(probs * prob_grad, axis=-1, keepdims=True)
        score_grad = (probs * (prob_grad - delta)).astype(BF16)
        dquery = jnp.einsum("rqk,rkd->rqd", score_grad, key_h, preferred_element_type=F32)
        dkey = jnp.einsum("rqk,rqd->rkd", score_grad, query_h, preferred_element_type=F32)
        dval = jnp.einsum("rqk,rqd->rkd", probs_low, grad_h, preferred_element_type=F32)
        scale = 1.0 / math.sqrt(DH)
        return (mix.astype(BF16), (dquery * scale).astype(BF16), (dkey * scale).astype(BF16), dval.astype(BF16))

    heads = tuple(split_heads(v) for v in (query, keys, vals, mix_grad))
    if query.shape[1] <= 512:
        return tuple(join_heads(v) for v in jax.vmap(head)(heads))
    count, rows = heads[0].shape[:2]
    place = jnp.tile(jnp.arange(rows), count)
    parts = tuple(v.reshape(count * rows, 1, *v.shape[2:]) for v in heads)
    done = lax.map(lambda p: head(p[0], query_seg[p[1]][None], key_seg[p[1]][None]), (parts, place))
    return tuple(join_heads(v.reshape(count, rows, *v.shape[2:])) for v in done)


def split_heads(value):
    rows, tokens, width = value.shape
    return value.reshape(rows, tokens, width // DH, DH).transpose(2, 0, 1, 3)


def join_heads(value):
    heads, rows, tokens, width = value.shape
    return value.transpose(1, 2, 0, 3).reshape(rows, tokens, heads * width)


def tokens_of(blocks):
    devices, rows, count, width = blocks.shape
    return blocks.transpose(1, 0, 2, 3).reshape(rows, devices * count, width)


def with_segment(rows, segs):
    marks = jnp.broadcast_to((segs + 2).astype(BF16)[..., None], segs.shape + (LANES,))
    return jnp.concatenate([rows, marks], axis=-1)


def local(
    tokens,
    segments,
    query_route,
    kv_route,
    ffn_route,
    grad_out,
    attn_gain,
    light_qkv,
    light_out,
    heavy_q,
    heavy_kv,
    heavy_out,
    route_query,
    ffn_gain,
    light_gate_up,
    light_down,
    heavy_gate_up,
    heavy_down,
    route_ffn,
):
    row_count, seg_span, width = tokens.shape
    light_heads = width // DL
    ffn_heavy = heavy_down.shape[0]
    devices = lax.axis_size("seq")
    me = lax.axis_index("seq")
    half_place = lax.axis_index("dp")
    anchor = me * seg_span
    routed_own = query_route.shape[1] // devices
    own_query = lax.dynamic_slice_in_dim(query_route, me * routed_own, routed_own, 1) - anchor
    own_key = lax.dynamic_slice_in_dim(kv_route, me * routed_own, routed_own, 1) - anchor
    own_ffn = ffn_route - anchor

    marked = with_segment(tokens, segments)
    before = shifted(marked[:, seg_span - RADIUS :], "seq", 1)
    after = shifted(marked[:, :RADIUS], "seq", -1)
    hidden = tokens.astype(F32)
    factor_one = rms_factor(hidden)
    normed = hidden * factor_one * attn_gain
    normed_low = normed.astype(BF16)
    key_rows = pick_rows(normed_low, own_key)
    key_payload = with_segment(key_rows, jnp.take_along_axis(segments, own_key, axis=1))
    key_blocks = tokens_of(gather_blocks(key_payload))
    key_all, key_seg = key_blocks[..., :width], key_blocks[..., width]

    extended = jnp.concatenate([before, marked, after], axis=1)
    seg_ext = extended[..., width]
    hidden_ext = extended[..., :width].astype(F32)
    factor_ext = rms_factor(hidden_ext)
    normed_ext_low = (hidden_ext * factor_ext * attn_gain).astype(BF16)
    extent = seg_span + 2 * RADIUS
    query_low = matmul(normed_low, light_qkv[:, :width]).astype(BF16)
    query_low = query_low.reshape(row_count, seg_span, light_heads, DL)
    kv_ext = matmul(normed_ext_low, light_qkv[:, width:]).astype(BF16)
    key_ext = kv_ext[..., :width].reshape(row_count, extent, light_heads, DL)
    val_ext = kv_ext[..., width:].reshape(row_count, extent, light_heads, DL)
    offset = jnp.arange(seg_span)[:, None] - jnp.arange(extent)[None, :] + RADIUS
    seg_own = seg_ext[:, RADIUS : RADIUS + seg_span]
    allowed = (jnp.abs(offset) <= RADIUS)[None] & (seg_own[:, :, None] == seg_ext[:, None, :])
    light_scale = 1.0 / math.sqrt(DL)
    scores = jnp.einsum("rqhd,rkhd->rhqk", query_low, key_ext, preferred_element_type=F32)
    scores = jnp.where(allowed[:, None], scores * light_scale, NEG_FILL)
    numerators = jnp.exp(scores - jnp.max(scores, axis=-1, keepdims=True))
    probs_light = numerators / jnp.sum(numerators, axis=-1, keepdims=True)
    probs_low = probs_light.astype(BF16)
    light_mix = jnp.einsum("rhqk,rkhd->rqhd", probs_low, val_ext, preferred_element_type=F32)
    light_mix = light_mix.reshape(row_count, seg_span, width).astype(BF16)
    light_attn = matmul(light_mix, light_out)

    query_rows = pick_rows(normed_low, own_query)
    query_seg_own = (jnp.take_along_axis(segments, own_query, axis=1) + 2).astype(BF16)
    heavy_query = matmul(query_rows, heavy_q).astype(BF16)
    keyval_all = matmul(key_all, heavy_kv).astype(BF16)
    heavy_width = heavy_q.shape[1]
    keys_all, vals_all = keyval_all[..., :heavy_width], keyval_all[..., heavy_width:]
    heavy_mix = heavy_forward(heavy_query, keys_all, vals_all, query_seg_own, key_seg)
    heavy_proj = matmul(heavy_mix, heavy_out)
    query_normed = pick_rows(normed, own_query)
    route_query_full = route_query.astype(F32)
    query_gate = jax.nn.sigmoid(jnp.sum(query_normed * route_query_full, axis=-1))
    heavy_attn = place_rows(query_gate[..., None] * heavy_proj, own_query, seg_span)

    middle = hidden + light_attn + heavy_attn
    factor_two = rms_factor(middle)
    normed_two = middle * factor_two * ffn_gain
    low_two = normed_two.astype(BF16)
    upstream = grad_out.astype(F32)
    ffn_normed = pick_rows(normed_two, own_ffn)
    ffn_rows = ffn_normed.astype(BF16)
    route_ffn_full = route_ffn.astype(F32)
    ffn_gate = jax.nn.sigmoid(jnp.sum(ffn_normed * route_ffn_full, axis=-1))
    ffn_upstream = pick_rows(upstream, own_ffn)
    ffn_low = (ffn_upstream * ffn_gate[..., None]).astype(BF16)
    routed_payload = with_segment(
        jnp.concatenate([ffn_rows, ffn_low, query_rows], axis=-1),
        jnp.take_along_axis(segments, own_query, axis=1),
    )
    routed_blocks = tokens_of(gather_blocks(routed_payload))
    ffn_all = routed_blocks[..., :width]
    ffn_low_all = routed_blocks[..., width : 2 * width]
    query_all = routed_blocks[..., 2 * width : 3 * width]
    query_seg = routed_blocks[..., 3 * width]

    hidden_light, gate_grad, up_grad = geglu(low_two, light_gate_up, light_down, grad_out)
    light_ff = matmul(hidden_light, light_down)
    light_both = jnp.concatenate([gate_grad, up_grad], axis=-1)
    normed_two_grad = matmul_t(light_both, light_gate_up)
    hidden_heavy, gate_grad_h, up_grad_h = geglu(ffn_rows, heavy_gate_up, heavy_down, ffn_low)
    heavy_ffn_proj = matmul(hidden_heavy, heavy_down)
    heavy_ff = place_rows(ffn_gate[..., None] * heavy_ffn_proj, own_ffn, seg_span)
    outputs = (middle + light_ff + heavy_ff).astype(BF16)
    ffn_gate_grad = jnp.sum(ffn_upstream * heavy_ffn_proj, axis=-1)
    ffn_logit_grad = ffn_gate_grad * ffn_gate * (1.0 - ffn_gate)
    route_ffn_grad = jnp.sum(ffn_logit_grad[..., None] * ffn_normed, axis=(0, 1))
    ffn_rows_grad = matmul_t(jnp.concatenate([gate_grad_h, up_grad_h], axis=-1), heavy_gate_up)
    ffn_rows_grad = ffn_rows_grad + ffn_logit_grad[..., None] * route_ffn_full
    normed_two_grad = normed_two_grad + place_rows(ffn_rows_grad, own_ffn, seg_span)
    ffn_gain_grad = jnp.sum(normed_two_grad * middle * factor_two, axis=(0, 1))
    middle_grad = upstream + norm_back(middle, factor_two, ffn_gain, normed_two_grad)
    middle_low = middle_grad.astype(BF16)

    valid_rows = (segments >= 0).astype(F32)[..., None]
    sums = jnp.stack(
        [
            jnp.sum(valid_rows * branch * branch)
            for branch in (hidden, light_attn, heavy_attn, light_ff, heavy_ff)
        ]
        + [jnp.sum(valid_rows)]
    )
    heavy_upstream = pick_rows(middle_grad, own_query)
    query_gate_grad = jnp.sum(heavy_upstream * heavy_proj, axis=-1)
    proj_low = (heavy_upstream * query_gate[..., None]).astype(BF16)
    sum_lanes = jnp.pad(jnp.concatenate(split_parts(sums)), (0, LANES - 18)).astype(BF16)
    sum_lanes = jnp.broadcast_to(sum_lanes, proj_low.shape[:2] + (LANES,))
    proj_blocks = gather_blocks(jnp.concatenate([proj_low, sum_lanes], axis=-1))
    sums_all = jnp.sum(proj_blocks[:, 0, 0, width : width + 18].astype(F32), axis=0)
    sums_all = jnp.sum(sums_all.reshape(3, 6), axis=0)
    sums_all = sums_all + swap(sums_all, "dp", 1)
    rms_stats = jnp.sqrt(sums_all[:5] / (sums_all[5] * width))
    proj_all = tokens_of(proj_blocks)[..., :width]

    flat = lambda v: v.reshape(-1, v.shape[-1])
    gate_up_grad = [
        jnp.dot(slot_columns(flat(low_two), me, devices).T, flat(part), preferred_element_type=F32)
        for part in own_half_first(light_both, half_place)
    ]
    hidden_slots = slot_columns(flat(hidden_light), me, devices).T
    down_grad = [
        jnp.dot(hidden_slots, flat(part), preferred_element_type=F32)
        for part in own_half_first(grad_out, half_place)
    ]
    mix_slots = slot_columns(flat(light_mix), me, devices).T
    out_grad = [
        jnp.dot(mix_slots, flat(part), preferred_element_type=F32)
        for part in own_half_first(middle_low, half_place)
    ]
    first_sum = scatter_sum(
        jnp.concatenate(
            [
                slot_block(gate_up_grad, devices),
                slot_block(down_grad, devices),
                slot_block(out_grad, devices),
                slot_vectors((ffn_gain_grad, route_ffn_grad), me, devices),
            ],
            axis=2,
        )
    )
    block = width // devices
    block_ff = light_down.shape[0] // devices
    cuts = [0]
    for rows in (
        block * light_gate_up.shape[1] // 2 // LANES,
        block_ff * width // 2 // LANES,
        block * width // 2 // LANES,
        block,
    ):
        cuts.append(cuts[-1] + rows)
    light_gate_up_grad = unslot(first_sum[cuts[0] : cuts[1]], light_gate_up.shape[1] // 2)
    light_down_grad = unslot(first_sum[cuts[1] : cuts[2]], width // 2)
    light_out_grad = unslot(first_sum[cuts[2] : cuts[3]], width // 2)
    ffn_gain_grad = first_sum[cuts[3] : cuts[4], 0]
    route_ffn_grad = first_sum[cuts[3] : cuts[4], 1]

    group = min(4, devices)
    low_place, high_place = me % group, me // group
    groups = devices // group
    unit = ffn_heavy // devices
    gate_up_parts = heavy_gate_up.reshape(width, 2, groups, group, unit)
    gate_up_mine = lax.dynamic_index_in_dim(gate_up_parts, low_place, 3, False)
    down_mine = lax.dynamic_index_in_dim(
        heavy_down.reshape(groups, group, unit, width), low_place, 1, False
    )
    x_all = flat(ffn_all)
    up_all = flat(ffn_low_all)
    hidden_mine, gate_mine, up_mine = geglu(
        x_all,
        gate_up_mine.reshape(width, -1),
        down_mine.reshape(-1, width),
        up_all,
    )
    hidden_block = lax.dynamic_slice_in_dim(hidden_mine, high_place * unit, unit, 1)
    heavy_down_half = [
        jnp.dot(hidden_block.T, part, preferred_element_type=F32)
        for part in own_half_first(up_all, half_place)
    ]
    heavy_down_grad = heavy_down_half[0] + swap(heavy_down_half[1].astype(BF16), "dp", 1).astype(F32)
    x_group = lax.dynamic_slice_in_dim(x_all, high_place * group * block, group * block, 1)
    x_group = x_group.reshape(-1, group, block)
    x_group = jnp.take(x_group, jnp.arange(group) ^ low_place, axis=1).reshape(-1, group * block)
    gate_half, up_half = (
        jnp.dot(x_group.T, part, preferred_element_type=F32) for part in (gate_mine, up_mine)
    )
    kept = jnp.where(half_place == 0, gate_half, up_half)
    sent = jnp.where(half_place == 0, up_half, gate_half)
    kept = (kept + swap(sent.astype(BF16), "dp", 1).astype(F32)).reshape(group, block, groups, unit)
    pieces = [kept[0]]
    for place in range(1, group):
        pieces.append(swap(kept[place].astype(BF16), "seq", place).astype(F32))
    pieces = jnp.take(jnp.stack(pieces, axis=2), jnp.arange(group) ^ low_place, axis=2)
    heavy_gate_up_grad = pieces.reshape(block, ffn_heavy)

    mix_grad = matmul_t(middle_low, light_out).astype(BF16)
    mix_grad = mix_grad.reshape(row_count, seg_span, light_heads, DL)
    val_grad = jnp.einsum("rhqk,rqhd->rkhd", probs_low, mix_grad, preferred_element_type=F32)
    prob_grad = jnp.einsum("rqhd,rkhd->rhqk", mix_grad, val_ext, preferred_element_type=F32)
    delta = jnp.sum(probs_light * prob_grad, axis=-1, keepdims=True)
    score_grad = (probs_light * (prob_grad - delta)).astype(BF16)
    query_grad = jnp.einsum("rhqk,rkhd->rqhd", score_grad, key_ext, preferred_element_type=F32)
    key_grad = jnp.einsum("rhqk,rqhd->rkhd", score_grad, query_low, preferred_element_type=F32)
    query_grad = (query_grad * light_scale).reshape(row_count, seg_span, width).astype(BF16)
    kv_grad = jnp.concatenate(
        [
            (key_grad * light_scale).reshape(row_count, extent, width),
            val_grad.reshape(row_count, extent, width),
        ],
        axis=-1,
    ).astype(BF16)
    normed_grad_ext = matmul_t(kv_grad, light_qkv[:, width:])
    normed_grad = matmul_t(query_grad, light_qkv[:, :width])
    normed_grad = normed_grad + normed_grad_ext[:, RADIUS : RADIUS + seg_span]
    from_right = shifted(normed_grad_ext[:, :RADIUS].astype(BF16), "seq", -1)
    from_left = shifted(normed_grad_ext[:, seg_span + RADIUS :].astype(BF16), "seq", 1)
    normed_grad = normed_grad.at[:, :RADIUS].add(from_left.astype(F32))
    normed_grad = normed_grad.at[:, seg_span - RADIUS :].add(from_right.astype(F32))

    hq_all = matmul(query_all, heavy_q).astype(BF16)
    do2_all = matmul_t(proj_all, heavy_out).astype(BF16)
    mix_all, dhq_all, dhk_all, dhv_all = heavy_both(
        hq_all, keys_all, vals_all, query_seg, key_seg, do2_all
    )
    dhkv_all = jnp.concatenate([dhk_all, dhv_all], axis=-1)
    mine = lambda v: lax.dynamic_slice_in_dim(flat(v), me * block, block, 1).T
    heavy_grads = [
        own_half_first(jnp.dot(mine(left), flat(right), preferred_element_type=F32), half_place)
        for left, right in ((query_all, dhq_all), (key_all, dhkv_all), (mix_all, proj_all))
    ]
    heavy_kept = jnp.concatenate([pair[0] for pair in heavy_grads], axis=-1)
    heavy_sent = jnp.concatenate([pair[1] for pair in heavy_grads], axis=-1)
    heavy_sum = heavy_kept + swap(heavy_sent.astype(BF16), "dp", 1).astype(F32)
    heavy_half = heavy_width // 2
    heavy_q_grad = heavy_sum[:, :heavy_half]
    heavy_kv_grad = heavy_sum[:, heavy_half : 3 * heavy_half]
    heavy_out_grad = heavy_sum[:, 3 * heavy_half :]
    query_logit_grad = query_gate_grad * query_gate * (1.0 - query_gate)
    route_query_grad = jnp.sum(query_logit_grad[..., None] * query_normed, axis=(0, 1))
    query_rows_grad = (
        matmul_t(dhq_all[:, :routed_own], heavy_q) + query_logit_grad[..., None] * route_query_full
    )
    key_rows_grad = matmul_t(dhkv_all[:, :routed_own], heavy_kv)
    normed_grad = (
        normed_grad
        + place_rows(query_rows_grad, own_query, seg_span)
        + place_rows(key_rows_grad, own_key, seg_span)
    )
    attn_gain_grad = jnp.sum(normed_grad * hidden * factor_one, axis=(0, 1))
    hidden_norm_grad = norm_back(hidden, factor_one, attn_gain, normed_grad)
    grad_tokens = (middle_grad + hidden_norm_grad).astype(BF16)

    own_slots = slot_columns(flat(normed_low), me, devices).T
    ext_slots = slot_columns(flat(normed_ext_low), me, devices).T
    qkv_grad = jnp.concatenate(
        [
            jnp.dot(own_slots, flat(query_grad), preferred_element_type=F32),
            jnp.dot(ext_slots, flat(kv_grad), preferred_element_type=F32),
        ],
        axis=-1,
    )
    second_sum = scatter_sum(
        jnp.concatenate(
            [
                slot_block(own_half_first(qkv_grad, half_place), devices),
                slot_vectors((attn_gain_grad, route_query_grad), me, devices),
            ],
            axis=2,
        )
    )
    qkv_cols = light_qkv.shape[1] // 2
    qkv_rows = block * qkv_cols // LANES
    light_qkv_grad = unslot(second_sum[:qkv_rows], qkv_cols)
    attn_gain_grad = second_sum[qkv_rows:, 0]
    route_query_grad = second_sum[qkv_rows:, 1]
    return (
        outputs,
        grad_tokens,
        attn_gain_grad,
        light_qkv_grad,
        light_out_grad,
        heavy_q_grad,
        heavy_kv_grad,
        heavy_out_grad,
        route_query_grad,
        ffn_gain_grad,
        light_gate_up_grad,
        light_down_grad,
        heavy_gate_up_grad,
        heavy_down_grad,
        route_ffn_grad,
        rms_stats,
    )


def solution(mesh):
    placed = (
        P("dp", "seq", None),
        P("dp", "seq"),
        P("dp", None),
        P("dp", None),
        P("dp", "seq"),
        P("dp", "seq", None),
    ) + (P(),) * 13
    matrix = P("seq", "dp")
    vector = P("seq")
    return jax.shard_map(
        local,
        mesh=mesh,
        in_specs=placed,
        out_specs=(
            P("dp", "seq", None),
            P("dp", "seq", None),
            vector,
            matrix,
            matrix,
            matrix,
            matrix,
            matrix,
            vector,
            vector,
            matrix,
            matrix,
            matrix,
            matrix,
            vector,
            P(),
        ),
        check_vma=False,
    )
```

time: 1390 us -> 507 us (0.36)
  waiting for transfers between devices: 884 us -> 57.7 us
  blocking collectives: 129 us -> 0 us
  local copies, waits for them, and re-layouts: 122 us -> 171 us
  starting transfers between devices: 11.5 us -> 45.2 us
  other arithmetic: 70.6 us -> 104 us
  matrix products: 144 us -> 119 us
    reduce_scatter x13 -> x0, waiting for transfers between devices: 856 us -> none  [the longest x1 236 us: local(): lax.psum_scatter(grad_terms[10], 'seq', scatter_dimension=0, tiled=True)]
    unnamed x1 -> x0, blocking collectives: 60.3 us -> none
    ppermute x2 -> x33, waiting for transfers between devices: 0.01 us -> 57.6 us  [swap(): lax.ppermute(value, axis, [(i, i ^ bit) for i in range(lax.axis_size(axis...]
    psum x2 -> x0, blocking collectives: 45.2 us -> none  [the longest x1 39.6 us: local(): lax.psum((squares, jnp.sum(valid_rows)), ('dp', 'seq'))]
    ppermute x2 -> x33, starting transfers between devices: 5.07 us -> 38 us  [swap(): lax.ppermute(value, axis, [(i, i ^ bit) for i in range(lax.axis_size(axis...]
    unnamed x26 -> x0, waiting for transfers between devices: 28 us -> none
    all_gather x1 -> x0, blocking collectives: 23.3 us -> none  [local(): seg_all = lax.all_gather(segments, 'seq', axis=1, tiled=True)]
    dot_general x38 -> x50, matrix products: 118 us -> 102 us  [the longest x12 27.3 us: matmul(): return jnp.einsum('...d,de->...e', left, right, preferred_element_type=F32)]
  transfers between devices with their start and end apart: 24 -> 37, of which waited for: 13 -> 13; matrix products, arithmetic and copies ran while one was open for 17% -> 50% of each run, Pallas kernels for 0% -> 0%
where the time goes in v1:
time: 507 us; the launch traced here: 500 us
  local copies, waits for them, and re-layouts  171 us (34%)
  matrix products  119 us (23%)
  other arithmetic  104 us (21%)
  waiting for transfers between devices  57.7 us (11%)
  starting transfers between devices  45.2 us (9%)
    ppermute x33, waiting for transfers between devices, swap(): lax.ppermute(value, axis, [(i, i ^ bit) for i in range(lax.axis_size(axis...  57.6 us
    unnamed x317, local copies, waits for them, and re-layouts  42.7 us
    ppermute x33, starting transfers between devices, swap(): lax.ppermute(value, axis, [(i, i ^ bit) for i in range(lax.axis_size(axis...  38 us
    dot_general x12, matrix products, matmul(): return jnp.einsum('...d,de->...e', left, right, preferred_element_type=F32)  27.3 us
    dot_general x11, matrix products, matmul_t(): return jnp.einsum('...e,de->...d', left, right, preferred_element_type=F32)  25.1 us
    gather x9, local copies, waits for them, and re-layouts, pick_rows(): return jnp.take_along_axis(source, positions[..., None], axis=1)  12.9 us
    convert_element_type x12, other arithmetic, add_halves(): (keep.astype(F32) + swap(sent, axis, bit).astype(F32)).astype(out_type)  10.9 us
    concatenate x9, other arithmetic, gather_blocks(): held = jnp.concatenate([held, swap(held, 'seq', bit)], axis=0)  10.2 us
  transfers between devices with their start and end apart: 37, of which 13 were waited for; matrix products, arithmetic and copies ran while one was open for 50% of the time, Pallas kernels for 0%

profile of v1, /device:TPU:0, one launch (start us, length us, event | category | flops | bytes accessed | tf_op | source)
XLA Modules:
  0.0 499.9 jit_solution(18322268782161776986)
XLA Ops:
  18.0 4.0 collective-permute-start.2
  54.0 16.9 %copy.201 = bf16[768,8192]{0,1:T(8,128)(2,1)} copy(bf16[768,8192]{1,0:T(8,128)(2,1)} %param.55) | data formatting | bytes 25165824 | tf_op args[16]
  70.9 3.8 constant_dynamic-slice_fusion
  82.8 4.6 collective-permute-start.3
  118.3 3.9 fusion.285
  156.0 7.5 %fusion.3 = f32[2,16,8192]{2,1,0:T(8,128)S(1)} fusion(bf16[2,16,768]{2,1,0:T(8,128)(2,1)S(1)} %select_convert_fusion.4, bf16[768,8192]{1,0:T(8,128)(2,1)} %param.55), kind=kOutput, calls=%fused_computation.15 | convolution fusion | flops 402653184 | bytes 13680640 | tf_op jit(solution)/shard_map/...d,de->...e/dot_general | solution.py:129
  163.6 4.1 multiply_reduce_fusion.8
  176.9 3.8 fusion.116
  188.2 3.9 stack.90
  218.1 4.8 fusion.286
  246.7 3.7 fusion.47
  250.4 3.7 select_convert_fusion.1
  254.1 3.5 stack.91
  257.6 5.2 %stack.92 = bf16[1,16,48,9,128]{4,3,2,1,0:T(8,128)(2,1)} reshape(bf16[768,1152]{1,0:T(8,128)(2,1)} %get-tuple-element.84) | data formatting | bytes 3538944 | tf_op jit(solution)/shard_map/stack | solution.py:85
  296.2 10.1 %collective-permute-done.10 = bf16[4,2,16,2432]{3,2,1,0:T(8,128)(2,1)S(1)} collective-permute-done((bf16[4,2,16,2432]{3,2,1,0:T(8,128)(2,1)S(1)}, bf16[4,2,16,2432]{3,2,1,0:T(8,128)(2,1)S(1)}, u32[]{:S(2)}, u32[]{:S(2)}) %collective-permute-start.10) | collective-permute-done | bytes 622624 | tf_op jit(solution)/shard_map/ppermute | solution.py:22
  367.6 4.7 fusion.136
  395.9 4.9 pad_maximum_fusion
  417.9 3.4 collective-permute-done.33
  426.9 3.7 add_convert_fusion
  447.6 4.7 collective-permute-done.18
  452.3 4.6 collective-permute-done.24
  459.0 10.1 %collective-permute-done.26 = bf16[8,1,384,128]{3,2,1,0:T(8,128)(2,1)S(1)} collective-permute-done((bf16[8,1,384,128]{3,2,1,0:T(8,128)(2,1)S(1)}, bf16[8,1,384,128]{3,2,1,0:T(8,128)(2,1)S(1)}, u32[]{:S(2)}, u32[]{:S(2)}) %collective-permute-start.26) | collective-permute-done | bytes 786464 | tf_op jit(solution)/shard_map/ppermute | solution.py:22
  479.9 8.1 %collective-permute-done.28 = bf16[2,1,768,128]{3,2,1,0:T(8,128)(2,1)S(1)} collective-permute-done((bf16[2,1,768,128]{3,2,1,0:T(8,128)(2,1)S(1)}, bf16[2,1,768,128]{3,2,1,0:T(8,128)(2,1)S(1)}, u32[]{:S(2)}, u32[]{:S(2)}) %collective-permute-start.28) | collective-permute-done | bytes 393248 | tf_op jit(solution)/shard_map/ppermute | solution.py:22
  491.1 5.8 %collective-permute-done.29 = bf16[1,1,768,128]{3,2,1,0:T(8,128)(2,1)S(1)} collective-permute-done((bf16[1,1,768,128]{3,2,1,0:T(8,128)(2,1)S(1)}, bf16[1,1,768,128]{3,2,1,0:T(8,128)(2,1)S(1)}, u32[]{:S(2)}, u32[]{:S(2)}) %collective-permute-start.29) | collective-permute-done | bytes 196640 | tf_op jit(solution)/shard_map/ppermute | solution.py:22
  (679 shorter events, 362.7 us)
Async XLA Ops:
  18.0 63.3 %collective-permute-start.2 = (bf16[1,2,16,896]{3,2,0,1:T(8,128)(2,1)}, bf16[1,2,16,896]{3,2,0,1:T(8,128)(2,1)}, u32[]{:S(2)}, u32[]{:S(2)}) collective-permute-start(bf16[1,2,16,896]{3,2,0,1:T(8,128)(2,1)} %maximum_bitcast_fusion.2), channel_id=1, source_target_pairs={{0,8},{1,9},{2,10},{3,11},{4,12},{5,13},{6,14},{7,15},{8,0},{9,1},... | collective-permute-start | bytes 172040 | tf_op jit(solution)/shard_map/ppermute | solution.py:22
  23.6 82.1 %collective-permute-start = (bf16[2,64,896]{2,1,0:T(8,128)(2,1)}, bf16[2,64,896]{2,1,0:T(8,128)(2,1)}, u32[]{:S(2)}, u32[]{:S(2)}) collective-permute-start(bf16[2,64,896]{2,1,0:T(8,128)(2,1)} %get-tuple-element.101), channel_id=1, source_target_pairs={{0,1},{1,2},{2,3},{3,4},{4,5},{5,6},{6,7},{7,8},{8,9},{9,10},{10,1... | collective-permute-start | bytes 688136 | tf_op jit(solution)/shard_map/ppermute | solution.py:28
  25.8 80.0 %collective-permute-start.1 = (bf16[2,64,896]{2,1,0:T(8,128)(2,1)}, bf16[2,64,896]{2,1,0:T(8,128)(2,1)}, u32[]{:S(2)}, u32[]{:S(2)}) collective-permute-start(bf16[2,64,896]{2,1,0:T(8,128)(2,1)} %get-tuple-element.102), channel_id=1, source_target_pairs={{1,0},{2,1},{3,2},{4,3},{5,4},{6,5},{7,6},{8,7},{9,8},{10,9},{11,1... | collective-permute-start | bytes 688136 | tf_op jit(solution)/shard_map/ppermute | solution.py:28
  82.8 19.1 %collective-permute-start.3 = (bf16[2,2,16,896]{3,2,0,1:T(8,128)(2,1)}, bf16[2,2,16,896]{3,2,0,1:T(8,128)(2,1)}, u32[]{:S(2)}, u32[]{:S(2)}) collective-permute-start(bf16[2,2,16,896]{3,2,0,1:T(8,128)(2,1)} %pad_maximum_fusion.19), channel_id=1, source_target_pairs={{0,4},{1,5},{2,6},{3,7},{4,0},{5,1},{6,2},{7,3},{8,12},{9,13},{10,... | collective-permute-start | bytes 344072 | tf_op jit(solution)/shard_map/ppermute | solution.py:22
  103.6 21.4 %collective-permute-start.4 = (bf16[4,2,16,896]{3,2,0,1:T(8,128)(2,1)}, bf16[4,2,16,896]{3,2,0,1:T(8,128)(2,1)}, u32[]{:S(2)}, u32[]{:S(2)}) collective-permute-start(bf16[4,2,16,896]{3,2,0,1:T(8,128)(2,1)} %pad_maximum_fusion.16), channel_id=1, source_target_pairs={{0,2},{1,3},{2,0},{3,1},{4,6},{5,7},{6,4},{7,5},{8,10},{9,11},{10,... | collective-permute-start | bytes 688136 | tf_op jit(solution)/shard_map/ppermute | solution.py:22
  206.3 75.4 %collective-permute-start.8 = (bf16[1,2,16,2432]{3,2,1,0:T(8,128)(2,1)}, bf16[1,2,16,2432]{3,2,1,0:T(8,128)(2,1)}, u32[]{:S(2)}, u32[]{:S(2)}) collective-permute-start(bf16[1,2,16,2432]{3,2,1,0:T(8,128)(2,1)} %maximum_bitcast_fusion.1), channel_id=1, source_target_pairs={{0,8},{1,9},{2,10},{3,11},{4,12},{5,13},{6,14},{7,15},{8,0},{9,1},... | collective-permute-start | bytes 466952 | tf_op jit(solution)/shard_map/ppermute | solution.py:22
  206.6 69.6 %collective-permute-start.12 = (bf16[1,2,16,896]{3,2,1,0:T(8,128)(2,1)}, bf16[1,2,16,896]{3,2,1,0:T(8,128)(2,1)}, u32[]{:S(2)}, u32[]{:S(2)}) collective-permute-start(bf16[1,2,16,896]{3,2,1,0:T(8,128)(2,1)} %maximum_bitcast_fusion.3), channel_id=1, source_target_pairs={{0,8},{1,9},{2,10},{3,11},{4,12},{5,13},{6,14},{7,15},{8,0},{9,1},... | collective-permute-start | bytes 172040 | tf_op jit(solution)/shard_map/ppermute | solution.py:22
  223.6 69.3 %collective-permute-start.6 = (bf16[2,64,768]{2,1,0:T(8,128)(2,1)}, bf16[2,64,768]{2,1,0:T(8,128)(2,1)}, u32[]{:S(2)}, u32[]{:S(2)}) collective-permute-start(bf16[2,64,768]{2,1,0:T(8,128)(2,1)} %get-tuple-element.98), channel_id=1, source_target_pairs={{0,1},{1,2},{2,3},{3,4},{4,5},{5,6},{6,7},{7,8},{8,9},{9,10},{10,1... | collective-permute-start | bytes 589832 | tf_op jit(solution)/shard_map/ppermute | solution.py:28
  226.2 67.8 %collective-permute-start.7 = (bf16[2,64,768]{2,1,0:T(8,128)(2,1)}, bf16[2,64,768]{2,1,0:T(8,128)(2,1)}, u32[]{:S(2)}, u32[]{:S(2)}) collective-permute-start(bf16[2,64,768]{2,1,0:T(8,128)(2,1)} %get-tuple-element.97), channel_id=1, source_target_pairs={{1,0},{2,1},{3,2},{4,3},{5,4},{6,5},{7,6},{8,7},{9,8},{10,9},{11,1... | collective-permute-start | bytes 589832 | tf_op jit(solution)/shard_map/ppermute | solution.py:28
  291.6 14.6 %collective-permute-start.10 = (bf16[4,2,16,2432]{3,2,1,0:T(8,128)(2,1)S(1)}, bf16[4,2,16,2432]{3,2,1,0:T(8,128)(2,1)S(1)}, u32[]{:S(2)}, u32[]{:S(2)}) collective-permute-start(bf16[4,2,16,2432]{3,2,1,0:T(8,128)(2,1)S(1)} %pad_maximum_fusion.9), channel_id=1, source_target_pairs={{0,2},{1,3},{2,0},{3,1},{4,6},{5,7},{6,4},{7,5},{8,10},{9,11},{10,... | collective-permute-start | bytes 1867784 | tf_op jit(solution)/shard_map/ppermute | solution.py:22
  296.0 12.2 %collective-permute-start.15 = (bf16[8,2,16,896]{3,2,1,0:T(8,128)(2,1)S(1)}, bf16[8,2,16,896]{3,2,1,0:T(8,128)(2,1)S(1)}, u32[]{:S(2)}, u32[]{:S(2)}) collective-permute-start(bf16[8,2,16,896]{3,2,1,0:T(8,128)(2,1)S(1)} %pad_maximum_fusion.11), channel_id=1, source_target_pairs={{0,1},{1,0},{2,3},{3,2},{4,5},{5,4},{6,7},{7,6},{8,9},{9,8},{10,11... | collective-permute-start | bytes 1376264 | tf_op jit(solution)/shard_map/ppermute | solution.py:22
  307.4 14.0 %collective-permute-start.11 = (bf16[8,2,16,2432]{3,2,1,0:T(8,128)(2,1)S(1)}, bf16[8,2,16,2432]{3,2,1,0:T(8,128)(2,1)}, u32[]{:S(2)}, u32[]{:S(2)}) collective-permute-start(bf16[8,2,16,2432]{3,2,1,0:T(8,128)(2,1)S(1)} %pad_maximum_fusion.5), channel_id=1, source_target_pairs={{0,1},{1,0},{2,3},{3,2},{4,5},{5,4},{6,7},{7,6},{8,9},{9,8},{10,11... | collective-permute-start | bytes 3735560 | tf_op jit(solution)/shard_map/ppermute | solution.py:22
  362.6 51.4 %collective-permute-start.35 = (bf16[256,384]{1,0:T(8,128)(2,1)}, bf16[256,384]{1,0:T(8,128)(2,1)}, u32[]{:S(2)}, u32[]{:S(2)}) collective-permute-start(bf16[256,384]{1,0:T(8,128)(2,1)} %convolution_convert_fusion.15), channel_id=1, source_target_pairs={{0,16},{16,0},{1,17},{17,1},{2,18},{18,2},{3,19},{19,3},{4,20},{20... | collective-permute-start | bytes 589832 | tf_op jit(solution)/shard_map/ppermute | solution.py:22
  375.3 36.4 %collective-permute-start.31 = (bf16[192,1024]{1,0:T(8,128)(2,1)}, bf16[192,1024]{1,0:T(8,128)(2,1)}, u32[]{:S(2)}, u32[]{:S(2)}) collective-permute-start(bf16[192,1024]{1,0:T(8,128)(2,1)} %get-tuple-element.151), channel_id=1, source_target_pairs={{0,16},{16,0},{1,17},{17,1},{2,18},{18,2},{3,19},{19,3},{4,20},{20... | collective-permute-start | bytes 1179656 | tf_op jit(solution)/shard_map/ppermute | solution.py:22
  378.5 30.8 %collective-permute-start.30 = (bf16[48,1536]{1,0:T(8,128)(2,1)}, bf16[48,1536]{1,0:T(8,128)(2,1)}, u32[]{:S(2)}, u32[]{:S(2)}) collective-permute-start(bf16[48,1536]{1,0:T(8,128)(2,1)} %pad_maximum_fusion.18), channel_id=1, source_target_pairs={{0,16},{16,0},{1,17},{17,1},{2,18},{18,2},{3,19},{19,3},{4,20},{20... | collective-permute-start | bytes 442376 | tf_op jit(solution)/shard_map/ppermute | solution.py:22
  404.3 22.6 %collective-permute-start.23 = (bf16[8,2,768,128]{3,2,1,0:T(8,128)(2,1)}, bf16[8,2,768,128]{3,2,1,0:T(8,128)(2,1)}, u32[]{:S(2)}, u32[]{:S(2)}) collective-permute-start(bf16[8,2,768,128]{3,2,1,0:T(8,128)(2,1)} %slice.500), channel_id=1, source_target_pairs={{0,1},{1,0},{2,3},{3,2},{4,5},{5,4},{6,7},{7,6},{8,9},{9,8},{10,11... | collective-permute-start | bytes 9437192 | tf_op jit(solution)/shard_map/ppermute | solution.py:22
  407.7 13.6 %collective-permute-start.16 = (bf16[8,2,480,128]{3,2,1,0:T(8,128)(2,1)}, bf16[8,2,480,128]{3,2,1,0:T(8,128)(2,1)}, u32[]{:S(2)}, u32[]{:S(2)}) collective-permute-start(bf16[8,2,480,128]{3,2,1,0:T(8,128)(2,1)} %pad_maximum_fusion.3), channel_id=1, source_target_pairs={{0,1},{1,0},{2,3},{3,2},{4,5},{5,4},{6,7},{7,6},{8,9},{9,8},{10,11... | collective-permute-start | bytes 5898248 | tf_op jit(solution)/shard_map/ppermute | solution.py:22
  425.7 16.3 %collective-permute-start.17 = (bf16[4,2,240,128]{3,2,1,0:T(8,128)(2,1)}, bf16[4,2,240,128]{3,2,1,0:T(8,128)(2,1)}, u32[]{:S(2)}, u32[]{:S(2)}) collective-permute-start(bf16[4,2,240,128]{3,2,1,0:T(8,128)(2,1)} %slice.484), channel_id=1, source_target_pairs={{0,2},{1,3},{2,0},{3,1},{4,6},{5,7},{6,4},{7,5},{8,10},{9,11},{10,... | collective-permute-start | bytes 1474568 | tf_op jit(solution)/shard_map/ppermute | solution.py:22
  426.3 19.2 %collective-permute-start.19 = (bf16[8,1,240,128]{3,2,1,0:T(8,128)(2,1)}, bf16[8,1,240,128]{3,2,1,0:T(8,128)(2,1)}, u32[]{:S(2)}, u32[]{:S(2)}) collective-permute-start(bf16[8,1,240,128]{3,2,1,0:T(8,128)(2,1)} %slice.488), channel_id=1, source_target_pairs={{0,16},{16,0},{1,17},{17,1},{2,18},{18,2},{3,19},{19,3},{4,20},{20... | collective-permute-start | bytes 1474568 | tf_op jit(solution)/shard_map/ppermute | solution.py:22
  431.5 25.5 %collective-permute-start.24 = (bf16[4,2,384,128]{3,2,1,0:T(8,128)(2,1)}, bf16[4,2,384,128]{3,2,1,0:T(8,128)(2,1)}, u32[]{:S(2)}, u32[]{:S(2)}) collective-permute-start(bf16[4,2,384,128]{3,2,1,0:T(8,128)(2,1)} %slice.502), channel_id=1, source_target_pairs={{0,2},{1,3},{2,0},{3,1},{4,6},{5,7},{6,4},{7,5},{8,10},{9,11},{10,... | collective-permute-start | bytes 2359304 | tf_op jit(solution)/shard_map/ppermute | solution.py:22
  444.9 24.2 %collective-permute-start.26 = (bf16[8,1,384,128]{3,2,1,0:T(8,128)(2,1)S(1)}, bf16[8,1,384,128]{3,2,1,0:T(8,128)(2,1)S(1)}, u32[]{:S(2)}, u32[]{:S(2)}) collective-permute-start(bf16[8,1,384,128]{3,2,1,0:T(8,128)(2,1)S(1)} %slice.506), channel_id=1, source_target_pairs={{0,16},{16,0},{1,17},{17,1},{2,18},{18,2},{3,19},{19,3},{4,20},{20... | collective-permute-start | bytes 2359304 | tf_op jit(solution)/shard_map/ppermute | solution.py:22
  446.8 23.2 %collective-permute-start.20 = (bf16[4,1,240,128]{3,2,1,0:T(8,128)(2,1)S(1)}, bf16[4,1,240,128]{3,2,1,0:T(8,128)(2,1)S(1)}, u32[]{:S(2)}, u32[]{:S(2)}) collective-permute-start(bf16[4,1,240,128]{3,2,1,0:T(8,128)(2,1)S(1)} %slice.490), channel_id=1, source_target_pairs={{0,2},{1,3},{2,0},{3,1},{4,6},{5,7},{6,4},{7,5},{8,10},{9,11},{10,... | collective-permute-start | bytes 737288 | tf_op jit(solution)/shard_map/ppermute | solution.py:22
  458.3 17.0 %collective-permute-start.25 = (bf16[4,1,384,128]{3,2,1,0:T(8,128)(2,1)S(1)}, bf16[4,1,384,128]{3,2,1,0:T(8,128)(2,1)S(1)}, u32[]{:S(2)}, u32[]{:S(2)}) collective-permute-start(bf16[4,1,384,128]{3,2,1,0:T(8,128)(2,1)S(1)} %slice.504), channel_id=1, source_target_pairs={{0,16},{16,0},{1,17},{17,1},{2,18},{18,2},{3,19},{19,3},{4,20},{20... | collective-permute-start | bytes 1179656 | tf_op jit(solution)/shard_map/ppermute | solution.py:22
  477.3 10.7 %collective-permute-start.28 = (bf16[2,1,768,128]{3,2,1,0:T(8,128)(2,1)S(1)}, bf16[2,1,768,128]{3,2,1,0:T(8,128)(2,1)S(1)}, u32[]{:S(2)}, u32[]{:S(2)}) collective-permute-start(bf16[2,1,768,128]{3,2,1,0:T(8,128)(2,1)S(1)} %pad_maximum_fusion.12), channel_id=1, source_target_pairs={{0,4},{1,5},{2,6},{3,7},{4,0},{5,1},{6,2},{7,3},{8,12},{9,13},{10,... | collective-permute-start | bytes 1179656 | tf_op jit(solution)/shard_map/ppermute | solution.py:22
  (162 other events, 994.1 us)

commit v2 on v1

--- a/solution.py
+++ b/solution.py
@@ -1,8 +1,11 @@
+import functools
 import math
 
 import jax
 import jax.numpy as jnp
 from jax import lax
+from jax.experimental import pallas as pl
+from jax.experimental.pallas import tpu as pltpu
 from jax.sharding import PartitionSpec as P
 
 DL = 96
@@ -214,7 +217,7 @@
     return jnp.concatenate([rows, marks], axis=-1)
 
 
-def local(
+def local_wide(
     tokens,
     segments,
     query_route,
@@ -533,6 +536,981 @@
         route_ffn_grad,
         rms_stats,
     )
+
+
+VMEM = pl.BlockSpec(memory_space=pltpu.VMEM)
+SMEM = pl.BlockSpec(memory_space=pltpu.SMEM)
+GELU_RATE = math.sqrt(2.0 / math.pi)
+GELU_CUBE = 0.044715
+VMEM_BYTES = 52 * 1024 * 1024
+
+
+def shape(dims, dtype):
+    return jax.ShapeDtypeStruct(dims, dtype)
+
+
+def call(kernel, outs, ins, smem=0, scratch=(), flops=0, moved=0):
+    return pl.pallas_call(
+        kernel,
+        out_shape=outs,
+        in_specs=[SMEM] * smem + [VMEM] * (len(ins) - smem),
+        out_specs=[VMEM] * len(outs),
+        scratch_shapes=list(scratch),
+        compiler_params=pltpu.CompilerParams(vmem_limit_bytes=VMEM_BYTES),
+        cost_estimate=pl.CostEstimate(flops=flops, bytes_accessed=moved, transcendentals=0),
+    )(*ins)
+
+
+def dot(left, right):
+    return jnp.dot(left, right, preferred_element_type=F32)
+
+
+def dot_t(left, right):
+    return lax.dot_general(left, right, (((1,), (1,)), ((), ())), preferred_element_type=F32)
+
+
+def t_dot(left, right):
+    return lax.dot_general(left, right, (((0,), (0,)), ((), ())), preferred_element_type=F32)
+
+
+def row_factor(value):
+    return lax.rsqrt(jnp.mean(value * value, axis=-1, keepdims=True) + EPSILON)
+
+
+def as_column(row):
+    count = row.shape[1]
+    down = lax.broadcasted_iota(jnp.int32, (count, count), 0)
+    along = lax.broadcasted_iota(jnp.int32, (count, count), 1)
+    return jnp.sum(jnp.where(down == along, row, 0.0), axis=1, keepdims=True)
+
+
+def head_window(head, size):
+    first = head * size // LANES * LANES
+    lanes = (head * size + size - 1) // LANES * LANES + LANES - first
+    place = lax.broadcasted_iota(jnp.int32, (1, lanes), 1) + first
+    return first, lanes, (place >= head * size) & (place < head * size + size)
+
+
+def slot_select(width, devices, me):
+    block = width // devices
+    bits = devices.bit_length() - 1
+    along = lax.broadcasted_iota(jnp.int32, (block, width), 1)
+    inside = lax.broadcasted_iota(jnp.int32, (block, width), 0)
+    rows = []
+    for p in range(devices):
+        owner = int(format(p, f"0{bits}b")[::-1], 2) ^ me
+        rows.append((along == inside + owner * block).astype(F32))
+    return jnp.concatenate(rows, axis=0).astype(BF16)
+
+
+def two_gelu(value):
+    square = value * value
+    bend = jnp.tanh(GELU_RATE * value * (1.0 + GELU_CUBE * square))
+    half = 0.5 * (1.0 + bend)
+    slope = half + 0.5 * value * (1.0 - bend * bend) * GELU_RATE * (1.0 + 3.0 * GELU_CUBE * square)
+    return value * half, slope
+
+
+def first_kernel(routed, route, seg_at, tokens, segs, gain, keys, upper, lower, normed, picked):
+    rows, span, width = tokens.shape
+    me = lax.axis_index("seq")
+    hidden = tokens[...].reshape(rows * span, width).astype(F32)
+    normed[...] = hidden * row_factor(hidden) * gain[...]
+    for r in range(rows):
+        for k in range(routed):
+            place = route[r, me * routed + k] - me * span
+            at = pl.ds(r * routed + k, 1)
+            picked[at, :width] = normed[pl.ds(r * span + place, 1), :]
+            picked[at, width:] = jnp.full((1, LANES), (seg_at[r, place] + 2).astype(F32))
+    keys[...] = picked[...].astype(BF16).reshape(keys.shape)
+    marks = (segs[...] + 2).astype(F32)
+    for out, start in ((upper, span - RADIUS), (lower, 0)):
+        out[:, :RADIUS, :] = tokens[:, start : start + RADIUS, :]
+        out[:, RADIUS:, :] = jnp.zeros((rows, 16, width), BF16)
+        for r in range(rows):
+            out[r, RADIUS:, :span] = jnp.broadcast_to(marks[r : r + 1], (16, span)).astype(BF16)
+
+
+def light_kernel(
+    before, tokens, after, segs, gain, w_qkv, w_out,
+    normed, query, keyval, probs, mix, attn, seg_row, mix_t,
+):
+    rows, span, width = tokens.shape
+    extent = span + 2 * RADIUS
+    heads = width // DL
+    for r in range(rows):
+        for part, at in ((before, 0), (tokens, RADIUS), (after, RADIUS + span)):
+            size = span if part is tokens else RADIUS
+            value = part[r, :size, :].astype(F32)
+            value = value * row_factor(value) * gain[...]
+            normed[r * extent + at : r * extent + at + size, :] = value.astype(BF16)
+    keyval[...] = dot(normed[...], w_qkv[:, width:]).astype(BF16)
+    own = [normed[r * extent + RADIUS : r * extent + RADIUS + span, :] for r in range(rows)]
+    query[...] = dot(jnp.concatenate(own, axis=0), w_qkv[:, :width]).astype(BF16)
+    down = lax.broadcasted_iota(jnp.int32, (extent, span), 0)
+    along = lax.broadcasted_iota(jnp.int32, (extent, span), 1)
+    near = jnp.abs(along - down + RADIUS) <= RADIUS
+    for r in range(rows):
+        marks = (segs[r : r + 1, :] + 2).astype(F32)
+        seg_row[:, :span] = before[r, RADIUS : RADIUS + 8, :span].astype(F32)
+        seg_row[:, span : 2 * span] = jnp.broadcast_to(marks, (8, span))
+        seg_row[:, 2 * span :] = after[r, RADIUS : RADIUS + 8, :span].astype(F32)
+        columns = [as_column(seg_row[0:1, c * span : (c + 1) * span]) for c in range(3)]
+        key_marks = jnp.concatenate([columns[0][span - RADIUS :], columns[1], columns[2][:RADIUS]], axis=0)
+        allowed = near & (key_marks == marks)
+        key_rows = slice(r * extent, (r + 1) * extent)
+        val_t = keyval[key_rows, width:].T
+        for h in range(heads):
+            first, lanes, mask = head_window(h, DL)
+            window = slice(first, first + lanes)
+            q_head = jnp.where(mask, query[r * span : (r + 1) * span, window], 0)
+            scores = dot_t(keyval[key_rows, window], q_head)
+            scores = jnp.where(allowed, scores * (1.0 / math.sqrt(DL)), NEG_FILL)
+            numer = jnp.exp(scores - jnp.max(scores, axis=0, keepdims=True))
+            share = (numer / jnp.sum(numer, axis=0, keepdims=True)).astype(BF16)
+            probs[r * heads + h] = share
+            mix_t[h * DL : (h + 1) * DL, :] = dot(val_t[h * DL : (h + 1) * DL, :], share)
+        mix[r * span : (r + 1) * span, :] = mix_t[...].T.astype(BF16)
+    attn[...] = dot(mix[...], w_out[...])
+
+
+def stat_row(value):
+    total = jnp.sum(jnp.sum(value, axis=0, keepdims=True), axis=1, keepdims=True)
+    return jnp.broadcast_to(total, (1, LANES))
+
+
+def valid_column(segs):
+    rows = segs.shape[0]
+    parts = [as_column((segs[r : r + 1, :] >= 0).astype(F32)) for r in range(rows)]
+    return jnp.concatenate(parts, axis=0)
+
+
+def router(rows, weights):
+    return jax.nn.sigmoid(jnp.sum(rows[...] * weights[...].astype(F32), axis=-1, keepdims=True))
+
+
+def middle_kernel(
+    routed, q_route, f_route, seg_at, tokens, segs, keys, attn, upstream, gain, ffn_gain,
+    w_q, w_kv, w_out, route_q, route_f,
+    middle, normed_two, keyval, payload, q_rows, f_rows, f_up, proj, f_marks, stats,
+    full, marks, placed,
+):
+    rows, span, width = tokens.shape
+    devices = keys.shape[0]
+    me = lax.axis_index("seq")
+    count = rows * routed
+    hidden = tokens[...].reshape(rows * span, width).astype(F32)
+    full[...] = hidden * row_factor(hidden) * gain[...]
+    for r in range(rows):
+        for k in range(routed):
+            at = pl.ds(r * routed + k, 1)
+            place = q_route[r, me * routed + k] - me * span
+            q_rows[at, :] = full[pl.ds(r * span + place, 1), :]
+            marks[at, :] = jnp.full((1, LANES), (seg_at[r, place] + 2).astype(F32))
+            place = f_route[r, k] - me * span
+            f_marks[at, :] = jnp.full((1, LANES), (seg_at[r, place] + 2).astype(F32))
+    q_low = q_rows[...].astype(BF16)
+    payload[:, :, 2 * width : 3 * width] = q_low.reshape(rows, routed, width)
+    payload[:, :, 3 * width :] = marks[...].astype(BF16).reshape(rows, routed, LANES)
+    key_low = keys[:, :, :, :width].reshape(devices * count, width)
+    keyval[...] = dot(key_low, w_kv[...]).astype(BF16).reshape(keyval.shape)
+    query = dot(q_low, w_q[...]).astype(BF16)
+    heads = width // DH
+    lane = lax.broadcasted_iota(jnp.int32, (1, width), 1)
+    masks = [(lane >= h * DH) & (lane < (h + 1) * DH) for h in range(heads)]
+    mixed = []
+    for r in range(rows):
+        mine = query[r * routed : (r + 1) * routed]
+        wide = jnp.concatenate([jnp.where(m, mine, 0) for m in masks], axis=0)
+        key_r = keyval[:, r, :, :width].reshape(devices * routed, width)
+        val_r = keyval[:, r, :, width:].reshape(devices * routed, width)
+        scores = dot_t(wide, key_r) * (1.0 / math.sqrt(DH))
+        key_marks = keys[:, r, :, width:].reshape(devices * routed, LANES).astype(F32).T[0:1, :]
+        query_marks = jnp.concatenate([marks[r * routed : (r + 1) * routed, 0:1]] * heads, axis=0)
+        scores = jnp.where(query_marks == key_marks, scores, NEG_FILL)
+        peak = jnp.maximum(jnp.max(scores, axis=-1, keepdims=True), 0.0)
+        numer = jnp.exp(scores - peak)
+        share = numer / (jnp.exp(-peak) + jnp.sum(numer, axis=-1, keepdims=True))
+        part = dot(share.astype(BF16), val_r)
+        total = jnp.zeros((routed, width), F32)
+        for h in range(heads):
+            total = total + jnp.where(masks[h], part[h * routed : (h + 1) * routed], 0.0)
+        mixed.append(total)
+    mixed = jnp.concatenate(mixed, axis=0).astype(BF16)
+    proj[...] = dot(mixed, w_out[...])
+    placed[...] = router(q_rows, route_q) * proj[...]
+    light = attn[...]
+    middle[...] = hidden + light
+    for r in range(rows):
+        for k in range(routed):
+            place = q_route[r, me * routed + k] - me * span
+            at = pl.ds(r * span + place, 1)
+            middle[at, :] = middle[at, :] + placed[pl.ds(r * routed + k, 1), :]
+    valid = valid_column(segs)
+    stats[...] = jnp.zeros(stats.shape, F32)
+    stats[0:1, :] = stat_row(valid * hidden * hidden)
+    stats[1:2, :] = stat_row(valid * light * light)
+    stats[2:3, :] = stat_row(jnp.where(marks[:, 0:1] >= 2.0, placed[...] * placed[...], 0.0))
+    stats[5:6, :] = stat_row(valid)
+    mid = middle[...]
+    full[...] = mid * row_factor(mid) * ffn_gain[...]
+    normed_two[...] = full[...].astype(BF16)
+    for r in range(rows):
+        for k in range(routed):
+            place = f_route[r, k] - me * span
+            f_rows[pl.ds(r * routed + k, 1), :] = full[pl.ds(r * span + place, 1), :]
+    full[...] = upstream[...].reshape(rows * span, width).astype(F32)
+    for r in range(rows):
+        for k in range(routed):
+            place = f_route[r, k] - me * span
+            f_up[pl.ds(r * routed + k, 1), :] = full[pl.ds(r * span + place, 1), :]
+    f_low = (router(f_rows, route_f) * f_up[...]).astype(BF16)
+    payload[:, :, :width] = f_rows[...].astype(BF16).reshape(rows, routed, width)
+    payload[:, :, width : 2 * width] = f_low.reshape(rows, routed, width)
+
+
+def glu_parts(inputs, back_in, gate_w, up_w, down_w):
+    act, slope = two_gelu(dot(inputs, gate_w))
+    lift = dot(inputs, up_w)
+    back = dot_t(back_in, down_w)
+    hidden = (act * lift).astype(BF16)
+    return hidden, (back * lift * slope).astype(BF16), (back * act).astype(BF16)
+
+
+def three_parts(value):
+    high = value.astype(BF16).astype(F32)
+    middle = (value - high).astype(BF16).astype(F32)
+    return high, middle, value - high - middle
+
+
+def ffn_kernel(
+    routed, q_route, f_route, normed_two, upstream, middle, w_gate, w_up, w_down,
+    h_gate, h_up, h_down, q_rows, f_rows, f_up, proj, f_marks, ffn_gain, route_q, route_f, stats, segs,
+    outputs, dmid, dmid_low, hidden_out, grad_gate, grad_up, payload, vectors,
+    z_light, d_light, z_heavy, d_heavy, placed, full,
+):
+    step = pl.program_id(0)
+    width = middle.shape[1]
+    rows, span = segs.shape
+    me = lax.axis_index("seq")
+
+    @pl.when(step == 0)
+    def _():
+        for total in (z_light, d_light, z_heavy, d_heavy):
+            total[...] = jnp.zeros(total.shape, F32)
+
+    grad = upstream[...].reshape(rows * span, width)
+    hidden, d_gate, d_up = glu_parts(normed_two[...], grad, w_gate[...], w_up[...], w_down[...])
+    hidden_out[...] = hidden
+    grad_gate[...] = d_gate
+    grad_up[...] = d_up
+    z_light[...] += dot(hidden, w_down[...])
+    d_light[...] += dot_t(d_gate, w_gate[...]) + dot_t(d_up, w_up[...])
+    f_gate = router(f_rows, route_f)
+    f_low = (f_gate * f_up[...]).astype(BF16)
+    f_in = f_rows[...].astype(BF16)
+    hidden, d_gate, d_up = glu_parts(f_in, f_low, h_gate[...], h_up[...], h_down[...])
+    z_heavy[...] += dot(hidden, h_down[...])
+    d_heavy[...] += dot_t(d_gate, h_gate[...]) + dot_t(d_up, h_up[...])
+
+    @pl.when(step == pl.num_programs(0) - 1)
+    def _():
+        mid = middle[...]
+        placed[...] = f_gate * z_heavy[...]
+        full[...] = mid + z_light[...]
+        logit = jnp.sum(f_up[...] * z_heavy[...], axis=-1, keepdims=True) * f_gate * (1.0 - f_gate)
+        d_heavy[...] += logit * route_f[...].astype(F32)
+        for r in range(rows):
+            for k in range(routed):
+                place = f_route[r, k] - me * span
+                at, source = pl.ds(r * span + place, 1), pl.ds(r * routed + k, 1)
+                full[at, :] = full[at, :] + placed[source, :]
+                d_light[at, :] = d_light[at, :] + d_heavy[source, :]
+        outputs[...] = full[...].astype(BF16).reshape(outputs.shape)
+        factor = row_factor(mid)
+        d_norm = d_light[...]
+        vectors[...] = jnp.zeros(vectors.shape, F32)
+        vectors[0:1, :] = jnp.sum(d_norm * mid * factor, axis=0, keepdims=True)
+        vectors[1:2, :] = jnp.sum(logit * f_rows[...], axis=0, keepdims=True)
+        weighted = d_norm * ffn_gain[...]
+        inner = jnp.mean(weighted * mid, axis=-1, keepdims=True)
+        total = grad.astype(F32) + factor * weighted - mid * (factor * factor * factor) * inner
+        dmid[...] = total
+        dmid_low[...] = total.astype(BF16)
+        sums = stats[...]
+        place = lax.broadcasted_iota(jnp.int32, sums.shape, 0)
+        lane = lax.broadcasted_iota(jnp.int32, sums.shape, 1)
+        light_sum = stat_row(valid_column(segs) * z_light[...] * z_light[...])
+        heavy_sum = stat_row(jnp.where(f_marks[:, 0:1] >= 2.0, placed[...] * placed[...], 0.0))
+        sums = jnp.where(place == 3, light_sum, jnp.where(place == 4, heavy_sum, sums))
+        lanes = jnp.zeros(sums.shape, F32)
+        for k, part in enumerate(three_parts(sums)):
+            lanes = lanes + jnp.where(lane == place + 8 * k, part, 0.0)
+        lanes = jnp.sum(lanes, axis=0, keepdims=True)
+        full[...] = total
+        for r in range(rows):
+            for k in range(routed):
+                place = q_route[r, me * routed + k] - me * span
+                placed[pl.ds(r * routed + k, 1), :] = full[pl.ds(r * span + place, 1), :]
+        q_gate = router(q_rows, route_q)
+        logit = jnp.sum(placed[...] * proj[...], axis=-1, keepdims=True) * q_gate * (1.0 - q_gate)
+        payload[:, :, :width] = (q_gate * placed[...]).astype(BF16).reshape(rows, routed, width)
+        lane = lax.broadcasted_iota(jnp.int32, (rows * routed, LANES), 1)
+        extra = jnp.broadcast_to(lanes, (rows * routed, LANES))
+        for k, part in enumerate(three_parts(logit)):
+            extra = jnp.where(lane == 24 + k, part, extra)
+        payload[:, :, width:] = extra.astype(BF16).reshape(rows, routed, LANES)
+
+
+def halves_of(value, place):
+    half = value.shape[-1] // 2
+    first, second = value[..., :half], value[..., half:]
+    return jnp.where(place == 0, first, second), jnp.where(place == 0, second, first)
+
+
+def store_slots(outs, place, base, grads):
+    kept, sent = outs
+    slots = kept.shape[0]
+    block = grads.shape[0] // (2 * slots)
+    low = grads.astype(BF16)
+    for c in range(grads.shape[1] // LANES):
+        for p in range(2 * slots):
+            part = low[p * block : (p + 1) * block, c * LANES : (c + 1) * LANES]
+            out = kept if p < slots else sent
+            out[p % slots, place, base + c * block : base + (c + 1) * block, :] = part
+    return base + grads.shape[1] // LANES * block
+
+
+def slot_vector_block(select, vectors):
+    table = jnp.concatenate([vectors, jnp.zeros((LANES - vectors.shape[0], vectors.shape[1]), F32)], axis=0)
+    return dot_t(select, table.astype(BF16))
+
+
+def first_grads_kernel(
+    normed_two, grad_gate, grad_up, hidden, upstream, mix, dmid_low, vectors, kept, sent
+):
+    devices = 2 * kept.shape[0]
+    width = normed_two.shape[1]
+    me = lax.axis_index("seq")
+    place = lax.axis_index("dp")
+    select = slot_select(width, devices, me)
+    inputs_t = dot_t(select, normed_two[...]).astype(BF16)
+    gate, up = grad_gate[...], grad_up[...]
+    ways = (jnp.where(place == 0, gate, up), jnp.where(place == 0, up, gate))
+    for half in range(2):
+        base = store_slots((kept, sent), half, 0, dot(inputs_t, ways[half]))
+    hidden_t = dot_t(slot_select(hidden.shape[1], devices, me), hidden[...]).astype(BF16)
+    ways = halves_of(upstream[...].reshape(-1, width), place)
+    for half in range(2):
+        base_two = store_slots((kept, sent), half, base, dot(hidden_t, ways[half]))
+    mix_t = dot_t(select, mix[...]).astype(BF16)
+    ways = halves_of(dmid_low[...], place)
+    for half in range(2):
+        base_three = store_slots((kept, sent), half, base_two, dot(mix_t, ways[half]))
+    table = slot_vector_block(select, vectors[...])
+    for half in range(2):
+        store_slots((kept, sent), half, base_three, table)
+
+
+def light_back_kernel(
+    dmid_low, query, keyval, probs, normed, gain, w_qkv, w_out,
+    dnorm, to_right, to_left, kept, sent, d_all, dkv, dq_t,
+):
+    rows, rim, width = to_right.shape
+    span = dmid_low.shape[0] // rows
+    extent = span + 2 * rim
+    heads = width // DL
+    scale = 1.0 / math.sqrt(DL)
+    me = lax.axis_index("seq")
+    place = lax.axis_index("dp")
+    mix_grad = dot_t(dmid_low[...], w_out[...]).astype(BF16)
+    for r in range(rows):
+        key_rows = slice(r * extent, (r + 1) * extent)
+        own_rows = slice(r * span, (r + 1) * span)
+        key_t = keyval[key_rows, :width].T
+        dkv[...] = jnp.zeros(dkv.shape, F32)
+        for h in range(heads):
+            first, lanes, mask = head_window(h, DL)
+            window = slice(first, first + lanes)
+            v_window = slice(width + first, width + first + lanes)
+            q_head = jnp.where(mask, query[own_rows, window], 0)
+            g_head = jnp.where(mask, mix_grad[own_rows, window], 0)
+            share = probs[r * heads + h]
+            full_share = share.astype(F32)
+            prob_grad = dot_t(keyval[key_rows, v_window], g_head)
+            delta = jnp.sum(full_share * prob_grad, axis=0, keepdims=True)
+            score_grad = (full_share * (prob_grad - delta)).astype(BF16)
+            dkv[:, window] += dot(score_grad, q_head)
+            dkv[:, v_window] += dot(share, g_head)
+            dq_t[h * DL : (h + 1) * DL, :] = dot(key_t[h * DL : (h + 1) * DL, :], score_grad)
+        d_all[key_rows, :width] = jnp.zeros((extent, width), BF16)
+        d_all[r * extent + rim : r * extent + rim + span, :width] = (dq_t[...].T * scale).astype(BF16)
+        d_all[key_rows, width : 2 * width] = (dkv[:, :width] * scale).astype(BF16)
+        d_all[key_rows, 2 * width :] = dkv[:, width:].astype(BF16)
+    d_norm = dot_t(d_all[...], w_qkv[...])
+    gain_grad = jnp.sum(d_norm * normed[...].astype(F32), axis=0, keepdims=True) / gain[...]
+    for r in range(rows):
+        to_left[r] = d_norm[r * extent : r * extent + rim].astype(BF16)
+        dnorm[r * span : (r + 1) * span, :] = d_norm[r * extent + rim : r * extent + rim + span]
+        to_right[r] = d_norm[r * extent + rim + span : (r + 1) * extent].astype(BF16)
+    select = slot_select(width, 2 * kept.shape[0], me)
+    inputs_t = dot_t(select, normed[...]).astype(BF16)
+    ways = halves_of(d_all[...], place)
+    table = slot_vector_block(select, jnp.broadcast_to(gain_grad, (8, width)))
+    for half in range(2):
+        base = store_slots((kept, sent), half, 0, dot(inputs_t, ways[half]))
+        store_slots((kept, sent), half, base, table)
+
+
+def heavy_ffn_kernel(
+    me_at, routed_all, h_gate, h_up, h_down, kept, sent, down_kept, down_sent, picked,
+):
+    step = pl.program_id(0)
+    devices, rows, routed, _ = routed_all.shape
+    width = h_gate.shape[0]
+    count = devices * rows * routed
+    me = me_at[0]
+    place = lax.axis_index("dp")
+    group = picked.shape[0] * devices // width
+    low_place = lax.rem(me, group)
+    high_place = lax.div(me, group)
+    block = width // devices
+    inputs = routed_all[:, :, :, :width].reshape(count, width)
+    back_in = routed_all[:, :, :, width : 2 * width].reshape(count, width)
+
+    @pl.when(step == 0)
+    def _():
+        along = lax.broadcasted_iota(jnp.int32, (block, width), 1)
+        inside = lax.broadcasted_iota(jnp.int32, (block, width), 0)
+        picks = []
+        for j in range(group):
+            owner = high_place * group + (low_place ^ j)
+            picks.append((along == inside + owner * block).astype(F32))
+        picked[...] = dot_t(jnp.concatenate(picks, axis=0).astype(BF16), inputs).astype(BF16)
+
+    hidden, d_gate, d_up = glu_parts(inputs, back_in, h_gate[...], h_up[...], h_down[...])
+    kept[...] = dot(picked[...], jnp.where(place == 0, d_gate, d_up))
+    sent[...] = dot(picked[...], jnp.where(place == 0, d_up, d_gate)).astype(BF16)
+
+    @pl.when(step == high_place)
+    def _():
+        hidden_t = hidden.T
+        mine, other = halves_of(back_in, place)
+        down_kept[...] = dot(hidden_t, mine)
+        down_sent[...] = dot(hidden_t, other).astype(BF16)
+
+
+def heavy_back_kernel(
+    routed, q_route, k_route, routed_all, proj_all, keyval, keys, dnorm, from_left, from_right, dmid, tokens,
+    gain, w_q, w_kv, w_out, route_q,
+    grad_tokens, kept, sent,
+    total, q_rows, k_rows, mix_t, dq_t, dkv,
+):
+    rows, span, width = tokens.shape
+    devices = keys.shape[0]
+    per_row = devices * routed
+    heads = width // DH
+    scale = 1.0 / math.sqrt(DH)
+    me = lax.axis_index("seq")
+    place = lax.axis_index("dp")
+    block = width // devices
+    along = lax.broadcasted_iota(jnp.int32, (block, width), 1)
+    inside = lax.broadcasted_iota(jnp.int32, (block, width), 0)
+    own_full = (along == inside + me * block).astype(F32)
+    own = own_full.astype(BF16)
+    q_grad = jnp.zeros((block, width), F32)
+    kv_grad = jnp.zeros((block, 2 * width), F32)
+    out_grad = jnp.zeros((block, width), F32)
+    route_grad = jnp.zeros((block, 1), F32)
+    for r in range(rows):
+        in_q = routed_all[:, r, :, 2 * width : 3 * width].reshape(per_row, width)
+        in_k = keys[:, r, :, :width].reshape(per_row, width)
+        q_marks = routed_all[:, r, :, 3 * width :].reshape(per_row, LANES).astype(F32).T[0:1, :]
+        k_marks = keys[:, r, :, width:].reshape(per_row, LANES).astype(F32)[:, 0:1]
+        allowed = k_marks == q_marks
+        grad_in = proj_all[:, r, :, :width].reshape(per_row, width)
+        extra = proj_all[:, r, :, width:].reshape(per_row, LANES).astype(F32)
+        extra_t = extra.T
+        query = dot(in_q, w_q[...]).astype(BF16)
+        mix_grad = dot_t(grad_in, w_out[...]).astype(BF16)
+        key_t = keyval[:, r, :, :width].reshape(per_row, width).T
+        val_t = keyval[:, r, :, width:].reshape(per_row, width).T
+        for first in range(0, width, LANES):
+            window = slice(first, first + LANES)
+            v_window = slice(width + first, width + first + LANES)
+            keys_w = keyval[:, r, :, window].reshape(per_row, LANES)
+            vals_w = keyval[:, r, :, v_window].reshape(per_row, LANES)
+            dk, dv = None, None
+            for h in range(first // DH, (first + LANES) // DH):
+                lane = lax.broadcasted_iota(jnp.int32, (1, LANES), 1) + first
+                mask = (lane >= h * DH) & (lane < (h + 1) * DH)
+                q_head = jnp.where(mask, query[:, window], 0)
+                g_head = jnp.where(mask, mix_grad[:, window], 0)
+                scores = jnp.where(allowed, dot_t(keys_w, q_head) * scale, NEG_FILL)
+                peak = jnp.maximum(jnp.max(scores, axis=0, keepdims=True), 0.0)
+                numer = jnp.exp(scores - peak)
+                share = numer / (jnp.exp(-peak) + jnp.sum(numer, axis=0, keepdims=True))
+                share_low = share.astype(BF16)
+                prob_grad = dot_t(vals_w, g_head)
+                delta = jnp.sum(share * prob_grad, axis=0, keepdims=True)
+                score_grad = (share * (prob_grad - delta)).astype(BF16)
+                at = slice(h * DH, (h + 1) * DH)
+                mix_t[at, :] = dot(val_t[at, :], share_low).astype(BF16)
+                dq_t[at, :] = dot(key_t[at, :], score_grad)
+                part_k, part_v = dot(score_grad, q_head), dot(share_low, g_head)
+                dk, dv = (part_k, part_v) if dk is None else (dk + part_k, dv + part_v)
+            dkv[:, window] = (dk * scale).astype(BF16)
+            dkv[:, v_window] = dv.astype(BF16)
+        dq = (dq_t[...].T * scale).astype(BF16)
+        in_q_t = dot_t(own, in_q)
+        q_grad = q_grad + dot(in_q_t.astype(BF16), dq)
+        kv_grad = kv_grad + dot(dot_t(own, in_k).astype(BF16), dkv[...])
+        out_grad = out_grad + dot(dot(own, mix_t[...]).astype(BF16), grad_in)
+        logit_row = extra_t[24:25, :] + extra_t[25:26, :] + extra_t[26:27, :]
+        route_grad = route_grad + jnp.sum(in_q_t * logit_row, axis=1, keepdims=True)
+        logit = extra[:routed, 24:25] + extra[:routed, 25:26] + extra[:routed, 26:27]
+        own_at = slice(r * routed, (r + 1) * routed)
+        q_rows[own_at, :] = dot_t(dq[:routed], w_q[...]) + logit * route_q[...].astype(F32)
+        k_rows[own_at, :] = dot_t(dkv[:routed, :], w_kv[...])
+        at = r * span
+        total[at : at + span, :] = dnorm[at : at + span, :]
+        total[at : at + RADIUS, :] += from_left[r].astype(F32)
+        total[at + span - RADIUS : at + span, :] += from_right[r].astype(F32)
+        for k in range(routed):
+            for route, part in ((q_route, q_rows), (k_route, k_rows)):
+                spot = route[r, me * routed + k] - me * span
+                row = pl.ds(at + spot, 1)
+                total[row, :] = total[row, :] + part[pl.ds(r * routed + k, 1), :]
+    hidden = tokens[...].reshape(rows * span, width).astype(F32)
+    factor = row_factor(hidden)
+    weighted = total[...] * gain[...]
+    inner = jnp.mean(weighted * hidden, axis=-1, keepdims=True)
+    d_hidden = dmid[...] + factor * weighted - hidden * (factor * factor * factor) * inner
+    grad_tokens[...] = d_hidden.astype(BF16).reshape(grad_tokens.shape)
+    own_gain = jnp.sum(own_full * gain[...], axis=1, keepdims=True)
+    own_route = jnp.sum(own_full * route_q[...].astype(F32), axis=1, keepdims=True)
+    gain_grad = jnp.sum(dot(own, w_q[...]) * q_grad, axis=1, keepdims=True)
+    gain_grad = gain_grad + jnp.sum(dot(own, w_kv[...]) * kv_grad, axis=1, keepdims=True)
+    gain_grad = (gain_grad + own_route * route_grad) / own_gain
+    lane = lax.broadcasted_iota(jnp.int32, (block, LANES), 1)
+    sums = jnp.sum(proj_all[:, 0, 0:1, width:].astype(F32), axis=0)
+    sums = jnp.broadcast_to(sums, (8, LANES))
+    sums = sums + pltpu.roll(sums, LANES - 8, 1) + pltpu.roll(sums, LANES - 16, 1)
+    sums = jnp.where(lane[:8] < 8, sums, 0.0)
+    vectors = jnp.where(lane == 0, gain_grad, jnp.where(lane == 1, route_grad, 0.0))
+    own_sums = pltpu.roll(sums, 8, 1)[0:1, :]
+    sent_sums = jnp.zeros((1, LANES), F32)
+    for k, part in enumerate(three_parts(sums)):
+        sent_sums = sent_sums + pltpu.roll(part, 8 + 8 * k, 1)[0:1, :]
+    at = 0
+    for grad in (q_grad, kv_grad, out_grad):
+        mine, other = halves_of(grad, place)
+        size = mine.shape[1]
+        kept[:, at : at + size] = mine
+        sent[:, at : at + size] = other.astype(BF16)
+        at += size
+    kept[:, at:] = vectors + own_sums
+    sent[:, at:] = (vectors + sent_sums).astype(BF16)
+
+
+def fold_kernel(pieces, count, *refs):
+    ins, outs = refs[: 2 * count], refs[2 * count :]
+    for out, parts in zip(outs, pieces):
+        for target, pair, index in parts:
+            value = ins[2 * pair][index].astype(F32) + ins[2 * pair + 1][index].astype(F32)
+            out[target] = value.astype(out.dtype)
+
+
+def finish_light_kernel(kept, received, *outs):
+    total = kept[0, 0].astype(F32) + received[0, 0].astype(F32)
+    base = 0
+    for ref in outs:
+        block = ref.shape[0]
+        for c in range(ref.shape[1] // LANES):
+            ref[:, c * LANES : (c + 1) * LANES] = total[base : base + block]
+            base += block
+
+
+def finish_heavy_kernel(
+    groups, heavy_kept, heavy_got, down_kept, down_got, own_piece, piece_one, piece_two, piece_three,
+    q_out, kv_out, out_out, vectors, stats, down_out, gate_up_out,
+):
+    me = lax.axis_index("seq")
+    total = heavy_kept[...] + heavy_got[...].astype(F32)
+    at = 0
+    for ref in (q_out, kv_out, out_out, vectors):
+        ref[...] = total[:, at : at + ref.shape[1]]
+        at += ref.shape[1]
+    sums = total[:8, at - LANES :]
+    stats[...] = sums + pltpu.roll(sums, LANES - 8, 1) + pltpu.roll(sums, LANES - 16, 1)
+    down_out[...] = down_kept[...] + down_got[...].astype(F32)
+    pieces = (own_piece, piece_one, piece_two, piece_three)
+    group = len(pieces)
+    low_place = lax.rem(me, group)
+    unit = own_piece.shape[1] // groups
+    for j, piece in enumerate(pieces):
+        for z in range(groups):
+            at = pl.multiple_of((z * group + (low_place ^ j)) * unit, unit)
+            gate_up_out[:, pl.ds(at, unit)] = piece[:, z * unit : (z + 1) * unit].astype(F32)
+
+
+def fold(pairs, outs):
+    flat = [ref for pair in pairs for ref in pair]
+    kernel = functools.partial(fold_kernel, [parts for _, _, parts in outs], len(pairs))
+    moved = sum(v.size * v.dtype.itemsize for v in flat)
+    return call(kernel, [shape(dims, dtype) for dims, dtype, _ in outs], flat, moved=2 * moved)
+
+
+def scatter_folds(kept, sent):
+    devices = lax.axis_size("seq")
+    slots, _, rows, _ = kept.shape
+    part, quarter = rows // 2, slots // 2
+    every = slice(None)
+    low, high = slice(0, part), slice(part, rows)
+    one, two = slice(0, 1), slice(1, 2)
+    near, far = slice(0, quarter), slice(quarter, slots)
+    left_keep, left_sent, right_keep, right_sent = fold(
+        [(kept, swap(sent, "seq", 1))],
+        [
+            ((quarter, 2, part, LANES), BF16, [(every, 0, (near, every, low))]),
+            ((quarter, 2, part, LANES), BF16, [(every, 0, (far, every, low))]),
+            ((slots, 1, part, LANES), BF16, [(every, 0, (every, one, high))]),
+            ((slots, 1, part, LANES), BF16, [(every, 0, (every, two, high))]),
+        ],
+    )
+    left_got, right_got = swap(left_sent, "seq", 2), swap(right_sent, "dp", 1)
+    left_keep, left_sent, right_keep, right_sent = fold(
+        [(left_keep, left_got), (right_keep, right_got)],
+        [
+            ((quarter, 1, part, LANES), BF16, [(every, 0, (every, one))]),
+            ((quarter, 1, part, LANES), BF16, [(every, 0, (every, two))]),
+            ((quarter, 1, part, LANES), BF16, [(every, 1, near)]),
+            ((quarter, 1, part, LANES), BF16, [(every, 1, far)]),
+        ],
+    )
+    left_got, right_got = swap(left_sent, "dp", 1), swap(right_sent, "seq", 2)
+    pairs = [(left_keep, left_got), (right_keep, right_got)]
+    count, bit = quarter, 4
+    while bit < devices:
+        half = count // 2
+        halves = (slice(0, half), slice(half, count))
+        if len(pairs) == 2:
+            wants = [
+                [((every, every, low), 0, side), ((every, every, high), 1, side)] for side in halves
+            ]
+        else:
+            wants = [[(every, 0, side)] for side in halves]
+        kept, sent = fold(pairs, [((half, 1, rows, LANES), BF16, want) for want in wants])
+        pairs = [(kept, swap(sent, "seq", bit))]
+        count, bit = half, 2 * bit
+    return pairs[0]
+
+
+def local_kernels(
+    tokens,
+    segments,
+    query_route,
+    kv_route,
+    ffn_route,
+    grad_out,
+    attn_gain,
+    light_qkv,
+    light_out,
+    heavy_q,
+    heavy_kv,
+    heavy_out,
+    route_query,
+    ffn_gain,
+    light_gate_up,
+    light_down,
+    heavy_gate_up,
+    heavy_down,
+    route_ffn,
+):
+    rows, span, width = tokens.shape
+    devices = lax.axis_size("seq")
+    routed = query_route.shape[1] // devices
+    own, count = rows * span, rows * routed
+    extent = span + 2 * RADIUS
+    block = width // devices
+    light_heads = width // DL
+    ffn_light, ffn_heavy = light_down.shape[0], heavy_down.shape[0]
+    attn_gain, ffn_gain, route_query, route_ffn = (
+        v.reshape(1, width) for v in (attn_gain, ffn_gain, route_query, route_ffn)
+    )
+    marked = width + LANES
+
+    rim = shape((rows, RADIUS + 16, width), BF16)
+    keys, upper, lower = call(
+        functools.partial(first_kernel, routed),
+        [shape((rows, routed, marked), BF16), rim, rim],
+        [kv_route, segments, tokens, segments, attn_gain],
+        smem=2,
+        scratch=[pltpu.VMEM((own, width), F32), pltpu.VMEM((count, marked), F32)],
+    )
+    before = shifted(upper, "seq", 1)
+    after = shifted(lower, "seq", -1)
+    keys_all = gather_blocks(keys)
+
+    normed, query, keyval, probs, mix, attn = call(
+        light_kernel,
+        [
+            shape((rows * extent, width), BF16),
+            shape((own, width), BF16),
+            shape((rows * extent, 2 * width), BF16),
+            shape((rows * light_heads, extent, span), BF16),
+            shape((own, width), BF16),
+            shape((own, width), F32),
+        ],
+        [before, tokens, after, segments, attn_gain, light_qkv, light_out],
+        scratch=[pltpu.VMEM((8, 3 * span), F32), pltpu.VMEM((width, span), F32)],
+        flops=4 * 10**9,
+        moved=8 * 10**6,
+    )
+
+    small = shape((count, width), F32)
+    middle, normed_two, keyval_all, payload, q_rows, f_rows, f_up, proj, f_marks, stats = call(
+        functools.partial(middle_kernel, routed),
+        [
+            shape((own, width), F32),
+            shape((own, width), BF16),
+            shape((devices, rows, routed, 2 * width), BF16),
+            shape((rows, routed, 3 * width + LANES), BF16),
+            small,
+            small,
+            small,
+            small,
+            shape((count, LANES), F32),
+            shape((8, LANES), F32),
+        ],
+        [
+            query_route, ffn_route, segments, tokens, segments, keys_all, attn, grad_out,
+            attn_gain, ffn_gain, heavy_q, heavy_kv, heavy_out, route_query, route_ffn,
+        ],
+        smem=3,
+        scratch=[
+            pltpu.VMEM((own, width), F32),
+            pltpu.VMEM((count, LANES), F32),
+            pltpu.VMEM((count, width), F32),
+        ],
+        flops=2 * 10**9,
+        moved=10**7,
+    )
+    routed_all = gather_blocks(payload)
+
+    steps = 4
+    whole = lambda *dims: pl.BlockSpec(dims, lambda j: (0,) * len(dims))
+    light_unit, heavy_unit = ffn_light // steps, ffn_heavy // steps
+    columns = lambda unit, at: pl.BlockSpec((width, unit), lambda j: (0, at + j))
+    downs = lambda unit: pl.BlockSpec((unit, width), lambda j: (j, 0))
+    share = pl.BlockSpec((own, light_unit), lambda j: (0, j))
+    outputs, dmid, dmid_low, hidden, grad_gate, grad_up, proj_payload, vectors = pl.pallas_call(
+        functools.partial(ffn_kernel, routed),
+        grid=(steps,),
+        out_shape=[
+            shape((rows, span, width), BF16),
+            shape((own, width), F32),
+            shape((own, width), BF16),
+            shape((own, ffn_light), BF16),
+            shape((own, ffn_light), BF16),
+            shape((own, ffn_light), BF16),
+            shape((rows, routed, marked), BF16),
+            shape((8, width), F32),
+        ],
+        in_specs=[
+            SMEM,
+            SMEM,
+            whole(own, width),
+            whole(rows, span, width),
+            whole(own, width),
+            columns(light_unit, 0),
+            columns(light_unit, steps),
+            downs(light_unit),
+            columns(heavy_unit, 0),
+            columns(heavy_unit, steps),
+            downs(heavy_unit),
+        ]
+        + [whole(count, width)] * 4
+        + [whole(count, LANES)]
+        + [whole(1, width)] * 3
+        + [whole(8, LANES), whole(rows, span)],
+        out_specs=[
+            whole(rows, span, width),
+            whole(own, width),
+            whole(own, width),
+            share,
+            share,
+            share,
+            whole(rows, routed, marked),
+            whole(8, width),
+        ],
+        scratch_shapes=[pltpu.VMEM((own, width), F32)] * 2
+        + [pltpu.VMEM((count, width), F32)] * 3
+        + [pltpu.VMEM((own, width), F32)],
+        compiler_params=pltpu.CompilerParams(vmem_limit_bytes=VMEM_BYTES),
+        cost_estimate=pl.CostEstimate(flops=10**10, bytes_accessed=3 * 10**7, transcendentals=0),
+    )(
+        query_route, ffn_route, normed_two, grad_out, middle, light_gate_up, light_gate_up, light_down,
+        heavy_gate_up, heavy_gate_up, heavy_down, q_rows, f_rows, f_up, proj, f_marks,
+        ffn_gain, route_query, route_ffn, stats, segments,
+    )
+    proj_all = gather_blocks(proj_payload)
+
+    slot_rows = (
+        block * ffn_light // LANES
+        + ffn_light // devices * (width // 2) // LANES
+        + block * (width // 2) // LANES
+        + block
+    )
+    slots = shape((devices // 2, 2, slot_rows, LANES), BF16)
+    kept, sent = call(
+        first_grads_kernel,
+        [slots, slots],
+        [normed_two, grad_gate, grad_up, hidden, grad_out, mix, dmid_low, vectors],
+        flops=3 * 10**9,
+        moved=8 * 10**6,
+    )
+    first_pair = scatter_folds(kept, sent)
+
+    slot_rows = block * (3 * width // 2) // LANES + block
+    slots = shape((devices // 2, 2, slot_rows, LANES), BF16)
+    rim = shape((rows, RADIUS, width), BF16)
+    dnorm, to_right, to_left, kept, sent = call(
+        light_back_kernel,
+        [shape((own, width), F32), rim, rim, slots, slots],
+        [dmid_low, query, keyval, probs, normed, attn_gain, light_qkv, light_out],
+        scratch=[
+            pltpu.VMEM((rows * extent, 3 * width), BF16),
+            pltpu.VMEM((extent, 2 * width), F32),
+            pltpu.VMEM((width, span), F32),
+        ],
+        flops=6 * 10**9,
+        moved=10**7,
+    )
+    from_left = shifted(to_right, "seq", 1)
+    from_right = shifted(to_left, "seq", -1)
+    second_pair = scatter_folds(kept, sent)
+
+    group = min(4, devices)
+    groups = devices // group
+    unit = ffn_heavy // devices
+    me = lax.axis_index("seq").astype(jnp.int32).reshape(1)
+    at_whole = lambda *dims: pl.BlockSpec(dims, lambda z, at: (0,) * len(dims))
+    hidden_block = lambda start: pl.BlockSpec(
+        (width, unit), lambda z, at: (0, start + z * group + lax.rem(at[0], group))
+    )
+    gate_kept, gate_sent, down_kept, down_sent = pl.pallas_call(
+        heavy_ffn_kernel,
+        grid_spec=pltpu.PrefetchScalarGridSpec(
+            num_scalar_prefetch=1,
+            grid=(groups,),
+            in_specs=[
+                at_whole(*routed_all.shape),
+                hidden_block(0),
+                hidden_block(devices),
+                pl.BlockSpec((unit, width), lambda z, at: (z * group + lax.rem(at[0], group), 0)),
+            ],
+            out_specs=[pl.BlockSpec((group * block, unit), lambda z, at: (0, z))] * 2
+            + [at_whole(unit, width // 2)] * 2,
+            scratch_shapes=[pltpu.VMEM((group * block, devices * count), BF16)],
+        ),
+        out_shape=[
+            shape((group * block, groups * unit), F32),
+            shape((group * block, groups * unit), BF16),
+            shape((unit, width // 2), F32),
+            shape((unit, width // 2), BF16),
+        ],
+        compiler_params=pltpu.CompilerParams(vmem_limit_bytes=VMEM_BYTES),
+        cost_estimate=pl.CostEstimate(flops=4 * 10**9, bytes_accessed=10**7, transcendentals=0),
+    )(me, routed_all, heavy_gate_up, heavy_gate_up, heavy_down)
+    down_got = swap(down_sent, "dp", 1)
+    rows_of = lambda j: slice(j * block, (j + 1) * block)
+    pieces = fold(
+        [(gate_kept, swap(gate_sent, "dp", 1))],
+        [
+            ((block, groups * unit), F32 if j == 0 else BF16, [(slice(None), 0, rows_of(j))])
+            for j in range(group)
+        ],
+    )
+    pieces = [pieces[0]] + [swap(pieces[j], "seq", j) for j in range(1, group)]
+
+    grad_tokens, heavy_kept, heavy_sent = call(
+        functools.partial(heavy_back_kernel, routed),
+        [
+            shape((rows, span, width), BF16),
+            shape((block, 2 * width + LANES), F32),
+            shape((block, 2 * width + LANES), BF16),
+        ],
+        [
+            query_route, kv_route, routed_all, proj_all, keyval_all, keys_all, dnorm, from_left, from_right,
+            dmid, tokens, attn_gain, heavy_q, heavy_kv, heavy_out, route_query,
+        ],
+        smem=2,
+        scratch=[
+            pltpu.VMEM((own, width), F32),
+            pltpu.VMEM((count, width), F32),
+            pltpu.VMEM((count, width), F32),
+            pltpu.VMEM((width, devices * routed), BF16),
+            pltpu.VMEM((width, devices * routed), F32),
+            pltpu.VMEM((devices * routed, 2 * width), BF16),
+        ],
+        flops=8 * 10**9,
+        moved=2 * 10**7,
+    )
+    heavy_got = swap(heavy_sent, "dp", 1)
+    heavy_q_grad, heavy_kv_grad, heavy_out_grad, heavy_vectors, stats, heavy_down_grad, heavy_gate_up_grad = call(
+        functools.partial(finish_heavy_kernel, groups),
+        [
+            shape((block, width // 2), F32),
+            shape((block, width), F32),
+            shape((block, width // 2), F32),
+            shape((block, LANES), F32),
+            shape((8, LANES), F32),
+            shape((unit, width // 2), F32),
+            shape((block, ffn_heavy), F32),
+        ],
+        [heavy_kept, heavy_got, down_kept, down_got, *pieces],
+    )
+    light_gate_up_grad, light_down_grad, light_out_grad, first_vectors = call(
+        finish_light_kernel,
+        [
+            shape((block, ffn_light), F32),
+            shape((ffn_light // devices, width // 2), F32),
+            shape((block, width // 2), F32),
+            shape((block, LANES), F32),
+        ],
+        first_pair,
+    )
+    light_qkv_grad, second_vectors = call(
+        finish_light_kernel,
+        [shape((block, 3 * width // 2), F32), shape((block, LANES), F32)],
+        second_pair,
+    )
+    sums = stats[0, 8:14]
+    return (
+        outputs,
+        grad_tokens,
+        second_vectors[:, 0] + heavy_vectors[:, 0],
+        light_qkv_grad,
+        light_out_grad,
+        heavy_q_grad,
+        heavy_kv_grad,
+        heavy_out_grad,
+        heavy_vectors[:, 1],
+        first_vectors[:, 0],
+        light_gate_up_grad,
+        light_down_grad,
+        heavy_gate_up_grad,
+        heavy_down_grad,
+        first_vectors[:, 1],
+        jnp.sqrt(sums[:5] / (sums[5] * width)),
+    )
+
+
+def local(tokens, segments, query_route, *others):
+    block = tokens.shape[2] // lax.axis_size("seq")
+    fits = query_route.shape[1] <= 256 and block % 16 == 0
+    return (local_kernels if fits else local_wide)(tokens, segments, query_route, *others)
 
 
 def solution(mesh):

time: 507 us -> 248 us (0.49)
  local copies, waits for them, and re-layouts: 171 us -> 16.7 us
  matrix products: 119 us -> 0 us
  Pallas kernels: 0 us -> 104 us
  other arithmetic: 104 us -> 2.83 us
  starting transfers between devices: 45.2 us -> 57.3 us
    dot_general x59 -> x0, matrix products: 115 us -> none  [the longest x12 27.3 us: matmul(): return jnp.einsum('...d,de->...e', left, right, preferred_element_type=F32)]
    pallas_call x0 -> x20, Pallas kernels: none -> 104 us  [the longest x18 75.8 us: call(): pl.pallas_call(kernel, out_shape=outs, in_specs=[SMEM] * smem + [VMEM] *...]
    unnamed x317 -> x50, local copies, waits for them, and re-layouts: 42.7 us -> 10.4 us
    gather x21 -> x0, local copies, waits for them, and re-layouts: 31.1 us -> none  [the longest x9 12.9 us: pick_rows(): return jnp.take_along_axis(source, positions[..., None], axis=1)]
    convert_element_type x28 -> x0, other arithmetic: 25.9 us -> none  [the longest x12 10.9 us: add_halves(): (keep.astype(F32) + swap(sent, axis, bit).astype(F32)).astype(out_type)]
    slice x35 -> x2, local copies, waits for them, and re-layouts: 26.3 us -> 1.28 us  [the longest x1 0.7 us: local_kernels(): first_vectors[:, 1]]
    convert_element_type x18 -> x0, local copies, waits for them, and re-layouts: 17.4 us -> none  [the longest x1 2.82 us: slot_block(): parts.transpose(1, 0, 3, 2, 4).reshape(devices, 2, -1, LANES).astype(BF16)]
    another operation x10 -> x0, local copies, waits for them, and re-layouts: 17.2 us -> none  [the longest x2 8.76 us: slot_block(): stacked = jnp.stack(grad_halves)]
  transfers between devices with their start and end apart: 37 -> 36, of which waited for: 13 -> 13; matrix products, arithmetic and copies ran while one was open for 50% -> 4% of each run, Pallas kernels for 0% -> 39%
where the time goes in v2:
time: 248 us; the launch traced here: 245 us
  Pallas kernels  104 us (42%)
  waiting for transfers between devices  61.8 us (25%)
  starting transfers between devices  57.3 us (23%)
  local copies, waits for them, and re-layouts  16.7 us (7%)
  other arithmetic  2.83 us (1%)
    pallas_call x18, Pallas kernels, call(): pl.pallas_call(kernel, out_shape=outs, in_specs=[SMEM] * smem + [VMEM] *...  75.8 us
    ppermute x32, waiting for transfers between devices, swap(): lax.ppermute(value, axis, [(i, i ^ bit) for i in range(lax.axis_size(axis...  61.8 us
    ppermute x32, starting transfers between devices, swap(): lax.ppermute(value, axis, [(i, i ^ bit) for i in range(lax.axis_size(axis...  51.6 us
    pallas_call x1, Pallas kernels, local_kernels(): pl.pallas_call(functools.partial(ffn_kernel, routed), grid=(steps,), out_...  19.8 us
    unnamed x50, local copies, waits for them, and re-layouts  10.4 us
    pallas_call x1, Pallas kernels, local_kernels(): pl.pallas_call(heavy_ffn_kernel, grid_spec=pltpu.PrefetchScalarGridSpec(n...  8.8 us
    ppermute x4, starting transfers between devices, shifted(): return lax.ppermute(block, axis, route)  5.72 us
  transfers between devices with their start and end apart: 36, of which 13 were waited for; matrix products, arithmetic and copies ran while one was open for 4% of the time, Pallas kernels for 39%

profile of v2, /device:TPU:0, one launch (start us, length us, event | category | flops | bytes accessed | tf_op | source)
XLA Modules:
  0.0 245.0 jit_solution(9525233293780130375)
XLA Ops:
  4.6 4.1 %collective-permute-start = (bf16[1,2,16,896]{3,2,1,0:T(8,128)(2,1)S(1)}, bf16[1,2,16,896]{3,2,1,0:T(8,128)(2,1)S(1)}, u32[]{:S(2)}, u32[]{:S(2)}) collective-permute-start(bf16[1,2,16,896]{3,2,1,0:T(8,128)(2,1)S(1)} %bitcast.18), channel_id=1, source_target_pairs={{0,8},{1,9},{2,10},{3,11},{4,12},{5,13},{6,14},{7,15},{8,0},{9,1},... | collective-permute-start | bytes 172040 | tf_op jit(solution)/shard_map/ppermute | solution.py:25
  8.7 2.8 %collective-permute-done = bf16[1,2,16,896]{3,2,1,0:T(8,128)(2,1)S(1)} collective-permute-done((bf16[1,2,16,896]{3,2,1,0:T(8,128)(2,1)S(1)}, bf16[1,2,16,896]{3,2,1,0:T(8,128)(2,1)S(1)}, u32[]{:S(2)}, u32[]{:S(2)}) %collective-permute-start) | collective-permute-done | bytes 57376 | tf_op jit(solution)/shard_map/ppermute | solution.py:25
  16.4 3.7 %collective-permute-start.2 = (bf16[4,2,16,896]{3,2,1,0:T(8,128)(2,1)S(1)}, bf16[4,2,16,896]{3,2,1,0:T(8,128)(2,1)S(1)}, u32[]{:S(2)}, u32[]{:S(2)}) collective-permute-start(bf16[4,2,16,896]{3,2,1,0:T(8,128)(2,1)S(1)} %pad_maximum_fusion.5), channel_id=1, source_target_pairs={{0,2},{1,3},{2,0},{3,1},{4,6},{5,7},{6,4},{7,5},{8,10},{9,11},{10,... | collective-permute-start | bytes 688136 | tf_op jit(solution)/shard_map/ppermute | solution.py:25
  22.2 6.4 %collective-permute-done.2 = bf16[4,2,16,896]{3,2,1,0:T(8,128)(2,1)S(1)} collective-permute-done((bf16[4,2,16,896]{3,2,1,0:T(8,128)(2,1)S(1)}, bf16[4,2,16,896]{3,2,1,0:T(8,128)(2,1)S(1)}, u32[]{:S(2)}, u32[]{:S(2)}) %collective-permute-start.2) | collective-permute-done | bytes 229408 | tf_op jit(solution)/shard_map/ppermute | solution.py:25
  28.9 10.0 %shard_map.307 = (bf16[512,768]{1,0:T(8,128)(2,1)}, bf16[256,768]{1,0:T(8,128)(2,1)S(1)}, bf16[512,1536]{1,0:T(8,128)(2,1)}, bf16[16,256,128]{2,1,0:T(8,128)(2,1...) custom-call(bf16[2,80,768]{2,1,0:T(8,128)(2,1)S(1)} %collective-permute-done.4.before, ...), custom_call_target="tpu_custom_call" | custom-call | flops 4000000000 | bytes 8000000 | tf_op jit(solution)/shard_map/pallas_call | solution.py:553
  39.9 7.7 %shard_map.308 = (f32[256,768]{1,0:T(8,128)}, bf16[256,768]{1,0:T(8,128)(2,1)S(1)}, bf16[16,2,16,1536]{3,2,1,0:T(8,128)(2,1)}, bf16[2,16,2432]{2,1,0:T(8,128)(2,...) custom-call(s32[2,256]{1,0:T(2,128)S(1)} %copy-done.7, ...), custom_call_target="tpu_custom_call" | custom-call | flops 2000000000 | bytes 10000000 | tf_op jit(solution)/shard_map/pallas_call | solution.py:553
  47.6 3.4 %collective-permute-start.6 = (bf16[1,2,16,2432]{3,2,1,0:T(8,128)(2,1)S(1)}, bf16[1,2,16,2432]{3,2,1,0:T(8,128)(2,1)S(1)}, u32[]{:S(2)}, u32[]{:S(2)}) collective-permute-start(bf16[1,2,16,2432]{3,2,1,0:T(8,128)(2,1)S(1)} %bitcast.10), channel_id=1, source_target_pairs={{0,8},{1,9},{2,10},{3,11},{4,12},{5,13},{6,14},{7,15},{8,0},{9,1},... | collective-permute-start | bytes 466952 | tf_op jit(solution)/shard_map/ppermute | solution.py:25
  50.9 19.8 %shard_map.309 = (bf16[2,128,768]{2,1,0:T(8,128)(2,1)}, f32[256,768]{1,0:T(8,128)}, bf16[256,768]{1,0:T(8,128)(2,1)S(1)}, bf16[256,1024]{1,0:T(8,128)(2,1)}, bf1...) custom-call(s32[2,256]{1,0:T(2,128)S(1)} %copy-done.7, ...), custom_call_target="tpu_custom_call" | custom-call | flops 10000000000 | bytes 30000000 | tf_op jit(solution)/shard_map/pallas_call | solution.py:1307
  70.7 8.2 %shard_map.320 = (bf16[8,2,768,128]{3,2,1,0:T(8,128)(2,1)}, bf16[8,2,768,128]{3,2,1,0:T(8,128)(2,1)}) custom-call(bf16[256,768]{1,0:T(8,128)(2,1)S(1)} %get-tuple-element.102.normed_two, bf16[256,1024]{1,0:T(8,128)(2,1)} %get-tuple-element.151.grad_gate, bf16[256,1024]{1,0:T(8,128)(2,1)} %get-tuple-element.152.grad_up, ...), custom_call_target="tpu_custom_call" | custom-call | flops 3000000000 | bytes 8000000 | tf_op jit(solution)/shard_map/pallas_call | solution.py:553
  80.2 9.9 %collective-permute-done.7 = bf16[2,2,16,2432]{3,2,1,0:T(8,128)(2,1)S(1)} collective-permute-done((bf16[2,2,16,2432]{3,2,1,0:T(8,128)(2,1)S(1)}, bf16[2,2,16,2432]{3,2,1,0:T(8,128)(2,1)S(1)}, u32[]{:S(2)}, u32[]{:S(2)}) %collective-permute-start.7) | collective-permute-done | bytes 311328 | tf_op jit(solution)/shard_map/ppermute | solution.py:25
  90.8 14.0 %shard_map.310 = (f32[256,768]{1,0:T(8,128)S(1)}, bf16[2,64,768]{2,1,0:T(8,128)(2,1)S(1)}, bf16[2,64,768]{2,1,0:T(8,128)(2,1)S(1)}, bf16[8,2,480,128]{3,2,1,0:T(8,128)(2,1)}, bf16[8,2,480,128]{3,2,1,0:T(8,128)(2,1)}) custom-call(bf16[256,768]{1,0:T(8,128)(2,1)S(1)} %get-tuple-element.114.dmid_low, bf16[256,768]{1,0:T(8,128)(2,1)S(1)} %get-tuple-element.115.query, ...), custom_call_target="tpu_custom_call" | custom-call | flops 6000000000 | bytes 10000000 | tf_op jit(solution)/shard_map/pallas_call | solution.py:553
  104.8 12.1 %collective-permute-start.11 = (bf16[2,2,16,896]{3,2,1,0:T(8,128)(2,1)S(1)}, bf16[2,2,16,896]{3,2,1,0:T(8,128)(2,1)S(1)}, u32[]{:S(2)}, u32[]{:S(2)}) collective-permute-start(bf16[2,2,16,896]{3,2,1,0:T(8,128)(2,1)S(1)} %pad_maximum_fusion.8), channel_id=1, source_target_pairs={{0,4},{1,5},{2,6},{3,7},{4,0},{5,1},{6,2},{7,3},{8,12},{9,13},{10,... | collective-permute-start | bytes 344072 | tf_op jit(solution)/shard_map/ppermute | solution.py:25
  118.2 4.3 %collective-permute-done.11 = bf16[2,2,16,896]{3,2,1,0:T(8,128)(2,1)S(1)} collective-permute-done((bf16[2,2,16,896]{3,2,1,0:T(8,128)(2,1)S(1)}, bf16[2,2,16,896]{3,2,1,0:T(8,128)(2,1)S(1)}, u32[]{:S(2)}, u32[]{:S(2)}) %collective-permute-start.11) | collective-permute-done | bytes 114720 | tf_op jit(solution)/shard_map/ppermute | solution.py:25
  125.9 3.9 %collective-permute-done.12 = bf16[4,2,16,896]{3,2,1,0:T(8,128)(2,1)S(1)} collective-permute-done((bf16[4,2,16,896]{3,2,1,0:T(8,128)(2,1)S(1)}, bf16[4,2,16,896]{3,2,1,0:T(8,128)(2,1)S(1)}, u32[]{:S(2)}, u32[]{:S(2)}) %collective-permute-start.12) | collective-permute-done | bytes 229408 | tf_op jit(solution)/shard_map/ppermute | solution.py:25
  132.3 4.3 %shard_map.321 = (bf16[4,2,384,128]{3,2,1,0:T(8,128)(2,1)S(1)}, bf16[4,2,384,128]{3,2,1,0:T(8,128)(2,1)S(1)}, bf16[8,1,384,128]{3,2,1,0:T(8,128)(2,1)}, bf16[8,1,384,128]{3,2,1,0:T(8,128)(2,1)}) custom-call(bf16[8,2,768,128]{3,2,1,0:T(8,128)(2,1)} %get-tuple-element.156.refs_0_, bf16[8,2,768,128]{3,2,1,0:T(8,128)(2,1)} %copy-done.12), custom_call_target="tpu_custom_call" | custom-call | bytes 12582912 | tf_op jit(solution)/shard_map/pallas_call | solution.py:553
  147.3 10.6 %collective-permute-done.30.refs_1_ = bf16[4,2,384,128]{3,2,1,0:T(8,128)(2,1)S(1)} collective-permute-done((bf16[4,2,384,128]{3,2,1,0:T(8,128)(2,1)S(1)}, bf16[4,2,384,128]{3,2,1,0:T(8,128)(2,1)S(1)}, u32[]{:S(2)}, u32[]{:S(2)}) %collective-permute-start.30) | collective-permute-done | bytes 786464 | tf_op jit(solution)/shard_map/ppermute | solution.py:25
  169.7 8.8 %shard_map.317 = (f32[192,1024]{1,0:T(8,128)S(1)}, bf16[192,1024]{1,0:T(8,128)(2,1)S(1)}, f32[256,384]{1,0:T(8,128)S(1)}, bf16[256,384]{1,0:T(8,128)(2,1)S(1)}) custom-call(s32[1]{0:T(128)} %bitcast.3.me_at, bf16[16,2,16,2432]{3,2,1,0:T(8,128)(2,1)} %copy-done.13, bf16[768,8192]{1,0:T(8,128)(2,1)} %h_up.3, bf16[768,8192]{1,0:T(8,128)(2,1)} %h_up.3, ...), custom_call_target="tpu_custom_call" | custom-call | flops 4000000000 | bytes 10000000 | tf_op jit(solution)/shard_map/pallas_call | solution.py:1402
  184.9 4.8 %collective-permute-start.20 = (bf16[4,1,240,128]{3,2,1,0:T(8,128)(2,1)S(1)}, bf16[4,1,240,128]{3,2,1,0:T(8,128)(2,1)S(1)}, u32[]{:S(2)}, u32[]{:S(2)}) collective-permute-start(bf16[4,1,240,128]{3,2,1,0:T(8,128)(2,1)S(1)} %get-tuple-element.133), channel_id=1, source_target_pairs={{0,2},{1,3},{2,0},{3,1},{4,6},{5,7},{6,4},{7,5},{8,10},{9,11},{10,... | collective-permute-start | bytes 737288 | tf_op jit(solution)/shard_map/ppermute | solution.py:25
  191.7 20.3 %shard_map.311 = (bf16[2,128,768]{2,1,0:T(8,128)(2,1)}, f32[48,1664]{1,0:T(8,128)S(1)}, bf16[48,1664]{1,0:T(8,128)(2,1)S(1)}) custom-call(s32[2,256]{1,0:T(2,128)S(1)} %copy-done.7, s32[2,256]{1,0:T(2,128)S(1)} %copy-done.9, bf16[16,2,16,2432]{3,2,1,0:T(8,128)(2,1)} %copy-done.13, bf16[16,2,16,896]{3,2,1,0:T(8,128)(2,1)} %constant_dynamic-update-slice_fusion.10.proj_all, ...), custom_call_target="tpu_custom_call" | custom-call | flops 8000000000 | bytes 20000000 | tf_op jit(solution)/shard_map/pallas_call | solution.py:553
  213.1 4.1 %collective-permute-done.23.heavy_got = bf16[48,1664]{1,0:T(8,128)(2,1)S(1)} collective-permute-done((bf16[48,1664]{1,0:T(8,128)(2,1)S(1)}, bf16[48,1664]{1,0:T(8,128)(2,1)S(1)}, u32[]{:S(2)}, u32[]{:S(2)}) %collective-permute-start.23) | collective-permute-done | bytes 159776 | tf_op jit(solution)/shard_map/ppermute | solution.py:25
  219.2 2.7 %collective-permute-done.27.piece_two = bf16[48,1024]{1,0:T(8,128)(2,1)S(1)} collective-permute-done((bf16[48,1024]{1,0:T(8,128)(2,1)S(1)}, bf16[48,1024]{1,0:T(8,128)(2,1)S(1)}, u32[]{:S(2)}, u32[]{:S(2)}) %collective-permute-start.27) | collective-permute-done | bytes 98336 | tf_op jit(solution)/shard_map/ppermute | solution.py:25
  226.6 3.0 %collective-permute-start.35 = (bf16[1,1,768,128]{3,2,1,0:T(8,128)(2,1)S(1)}, bf16[1,1,768,128]{3,2,1,0:T(8,128)(2,1)S(1)}, u32[]{:S(2)}, u32[]{:S(2)}) collective-permute-start(bf16[1,1,768,128]{3,2,1,0:T(8,128)(2,1)S(1)} %get-tuple-element.169), channel_id=1, source_target_pairs={{0,8},{1,9},{2,10},{3,11},{4,12},{5,13},{6,14},{7,15},{8,0},{9,1},... | collective-permute-start | bytes 589832 | tf_op jit(solution)/shard_map/ppermute | solution.py:25
  230.2 9.0 %collective-permute-done.22.received = bf16[1,1,480,128]{3,2,1,0:T(8,128)(2,1)S(1)} collective-permute-done((bf16[1,1,480,128]{3,2,1,0:T(8,128)(2,1)S(1)}, bf16[1,1,480,128]{3,2,1,0:T(8,128)(2,1)S(1)}, u32[]{:S(2)}, u32[]{:S(2)}) %collective-permute-start.22) | collective-permute-done | bytes 122912 | tf_op jit(solution)/shard_map/ppermute | solution.py:25
  240.6 2.7 %collective-permute-done.35.received = bf16[1,1,768,128]{3,2,1,0:T(8,128)(2,1)S(1)} collective-permute-done((bf16[1,1,768,128]{3,2,1,0:T(8,128)(2,1)S(1)}, bf16[1,1,768,128]{3,2,1,0:T(8,128)(2,1)S(1)}, u32[]{:S(2)}, u32[]{:S(2)}) %collective-permute-start.35) | collective-permute-done | bytes 196640 | tf_op jit(solution)/shard_map/ppermute | solution.py:25
  (138 shorter events, 62.6 us)
Async XLA Ops:
  12.8 16.0 %collective-permute-start.4 = (bf16[2,80,768]{2,1,0:T(8,128)(2,1)S(1)}, bf16[2,80,768]{2,1,0:T(8,128)(2,1)S(1)}, u32[]{:S(2)}, u32[]{:S(2)}) collective-permute-start(bf16[2,80,768]{2,1,0:T(8,128)(2,1)S(1)} %get-tuple-element.99), channel_id=1, source_target_pairs={{0,1},{1,2},{2,3},{3,4},{4,5},{5,6},{6,7},{7,8},{8,9},{9,10},{10,1... | collective-permute-start | bytes 737288 | tf_op jit(solution)/shard_map/ppermute | solution.py:31
  14.1 14.7 %collective-permute-start.5 = (bf16[2,80,768]{2,1,0:T(8,128)(2,1)S(1)}, bf16[2,80,768]{2,1,0:T(8,128)(2,1)S(1)}, u32[]{:S(2)}, u32[]{:S(2)}) collective-permute-start(bf16[2,80,768]{2,1,0:T(8,128)(2,1)S(1)} %get-tuple-element.100), channel_id=1, source_target_pairs={{1,0},{2,1},{3,2},{4,3},{5,4},{6,5},{7,6},{8,7},{9,8},{10,9},{11,1... | collective-permute-start | bytes 737288 | tf_op jit(solution)/shard_map/ppermute | solution.py:31
  47.6 31.5 %collective-permute-start.6 = (bf16[1,2,16,2432]{3,2,1,0:T(8,128)(2,1)S(1)}, bf16[1,2,16,2432]{3,2,1,0:T(8,128)(2,1)S(1)}, u32[]{:S(2)}, u32[]{:S(2)}) collective-permute-start(bf16[1,2,16,2432]{3,2,1,0:T(8,128)(2,1)S(1)} %bitcast.10), channel_id=1, source_target_pairs={{0,8},{1,9},{2,10},{3,11},{4,12},{5,13},{6,14},{7,15},{8,0},{9,1},... | collective-permute-start | bytes 466952 | tf_op jit(solution)/shard_map/ppermute | solution.py:25
  78.9 51.7 %collective-permute-start.29 = (bf16[8,2,768,128]{3,2,1,0:T(8,128)(2,1)}, bf16[8,2,768,128]{3,2,1,0:T(8,128)(2,1)S(1)}, u32[]{:S(2)}, u32[]{:S(2)}) collective-permute-start(bf16[8,2,768,128]{3,2,1,0:T(8,128)(2,1)} %get-tuple-element.157), channel_id=1, source_target_pairs={{0,1},{1,0},{2,3},{3,2},{4,5},{5,4},{6,7},{7,6},{8,9},{9,8},{10,11... | collective-permute-start | bytes 9437192 | tf_op jit(solution)/shard_map/ppermute | solution.py:25
  79.2 25.6 %collective-permute-start.10 = (bf16[1,2,16,896]{3,2,1,0:T(8,128)(2,1)S(1)}, bf16[1,2,16,896]{3,2,1,0:T(8,128)(2,1)S(1)}, u32[]{:S(2)}, u32[]{:S(2)}) collective-permute-start(bf16[1,2,16,896]{3,2,1,0:T(8,128)(2,1)S(1)} %bitcast.14), channel_id=1, source_target_pairs={{0,8},{1,9},{2,10},{3,11},{4,12},{5,13},{6,14},{7,15},{8,0},{9,1},... | collective-permute-start | bytes 172040 | tf_op jit(solution)/shard_map/ppermute | solution.py:25
  90.1 33.9 %collective-permute-start.8 = (bf16[4,2,16,2432]{3,2,1,0:T(8,128)(2,1)S(1)}, bf16[4,2,16,2432]{3,2,1,0:T(8,128)(2,1)S(1)}, u32[]{:S(2)}, u32[]{:S(2)}) collective-permute-start(bf16[4,2,16,2432]{3,2,1,0:T(8,128)(2,1)S(1)} %pad_maximum_fusion.1), channel_id=1, source_target_pairs={{0,2},{1,3},{2,0},{3,1},{4,6},{5,7},{6,4},{7,5},{8,10},{9,11},{10,... | collective-permute-start | bytes 1867784 | tf_op jit(solution)/shard_map/ppermute | solution.py:25
  104.8 38.4 %collective-permute-start.16 = (bf16[8,2,480,128]{3,2,1,0:T(8,128)(2,1)}, bf16[8,2,480,128]{3,2,1,0:T(8,128)(2,1)}, u32[]{:S(2)}, u32[]{:S(2)}) collective-permute-start(bf16[8,2,480,128]{3,2,1,0:T(8,128)(2,1)} %get-tuple-element.125), channel_id=1, source_target_pairs={{0,1},{1,0},{2,3},{3,2},{4,5},{5,4},{6,7},{7,6},{8,9},{9,8},{10,11... | collective-permute-start | bytes 5898248 | tf_op jit(solution)/shard_map/ppermute | solution.py:25
  104.8 17.6 %collective-permute-start.11 = (bf16[2,2,16,896]{3,2,1,0:T(8,128)(2,1)S(1)}, bf16[2,2,16,896]{3,2,1,0:T(8,128)(2,1)S(1)}, u32[]{:S(2)}, u32[]{:S(2)}) collective-permute-start(bf16[2,2,16,896]{3,2,1,0:T(8,128)(2,1)S(1)} %pad_maximum_fusion.8), channel_id=1, source_target_pairs={{0,4},{1,5},{2,6},{3,7},{4,0},{5,1},{6,2},{7,3},{8,12},{9,13},{10,... | collective-permute-start | bytes 344072 | tf_op jit(solution)/shard_map/ppermute | solution.py:25
  125.2 38.3 %collective-permute-start.9 = (bf16[8,2,16,2432]{3,2,1,0:T(8,128)(2,1)}, bf16[8,2,16,2432]{3,2,1,0:T(8,128)(2,1)}, u32[]{:S(2)}, u32[]{:S(2)}) collective-permute-start(bf16[8,2,16,2432]{3,2,1,0:T(8,128)(2,1)} %pad_maximum_fusion), channel_id=1, source_target_pairs={{0,1},{1,0},{2,3},{3,2},{4,5},{5,4},{6,7},{7,6},{8,9},{9,8},{10,11... | collective-permute-start | bytes 3735560 | tf_op jit(solution)/shard_map/ppermute | solution.py:25
  137.6 20.3 %collective-permute-start.30 = (bf16[4,2,384,128]{3,2,1,0:T(8,128)(2,1)S(1)}, bf16[4,2,384,128]{3,2,1,0:T(8,128)(2,1)S(1)}, u32[]{:S(2)}, u32[]{:S(2)}) collective-permute-start(bf16[4,2,384,128]{3,2,1,0:T(8,128)(2,1)S(1)} %get-tuple-element.159), channel_id=1, source_target_pairs={{0,2},{1,3},{2,0},{3,1},{4,6},{5,7},{6,4},{7,5},{8,10},{9,11},{10,... | collective-permute-start | bytes 2359304 | tf_op jit(solution)/shard_map/ppermute | solution.py:25
  139.0 20.4 %collective-permute-start.31 = (bf16[8,1,384,128]{3,2,1,0:T(8,128)(2,1)}, bf16[8,1,384,128]{3,2,1,0:T(8,128)(2,1)S(1)}, u32[]{:S(2)}, u32[]{:S(2)}) collective-permute-start(bf16[8,1,384,128]{3,2,1,0:T(8,128)(2,1)} %get-tuple-element.161), channel_id=1, source_target_pairs={{0,16},{16,0},{1,17},{17,1},{2,18},{18,2},{3,19},{19,3},{4,20},{20... | collective-permute-start | bytes 2359304 | tf_op jit(solution)/shard_map/ppermute | solution.py:25
  140.6 44.3 %collective-permute-start.14 = (bf16[2,64,768]{2,1,0:T(8,128)(2,1)S(1)}, bf16[2,64,768]{2,1,0:T(8,128)(2,1)S(1)}, u32[]{:S(2)}, u32[]{:S(2)}) collective-permute-start(bf16[2,64,768]{2,1,0:T(8,128)(2,1)S(1)} %get-tuple-element.120), channel_id=1, source_target_pairs={{0,1},{1,2},{2,3},{3,4},{4,5},{5,6},{6,7},{7,8},{8,9},{9,10},{10,1... | collective-permute-start | bytes 589832 | tf_op jit(solution)/shard_map/ppermute | solution.py:31
  146.6 21.8 %collective-permute-start.17 = (bf16[4,2,240,128]{3,2,1,0:T(8,128)(2,1)S(1)}, bf16[4,2,240,128]{3,2,1,0:T(8,128)(2,1)S(1)}, u32[]{:S(2)}, u32[]{:S(2)}) collective-permute-start(bf16[4,2,240,128]{3,2,1,0:T(8,128)(2,1)S(1)} %get-tuple-element.127), channel_id=1, source_target_pairs={{0,2},{1,3},{2,0},{3,1},{4,6},{5,7},{6,4},{7,5},{8,10},{9,11},{10,... | collective-permute-start | bytes 1474568 | tf_op jit(solution)/shard_map/ppermute | solution.py:25
  157.9 20.7 %collective-permute-start.18 = (bf16[8,1,240,128]{3,2,1,0:T(8,128)(2,1)S(1)}, bf16[8,1,240,128]{3,2,1,0:T(8,128)(2,1)S(1)}, u32[]{:S(2)}, u32[]{:S(2)}) collective-permute-start(bf16[8,1,240,128]{3,2,1,0:T(8,128)(2,1)S(1)} %get-tuple-element.129), channel_id=1, source_target_pairs={{0,16},{16,0},{1,17},{17,1},{2,18},{18,2},{3,19},{19,3},{4,20},{20... | collective-permute-start | bytes 1474568 | tf_op jit(solution)/shard_map/ppermute | solution.py:25
  162.5 19.1 %collective-permute-start.32 = (bf16[4,1,384,128]{3,2,1,0:T(8,128)(2,1)S(1)}, bf16[4,1,384,128]{3,2,1,0:T(8,128)(2,1)S(1)}, u32[]{:S(2)}, u32[]{:S(2)}) collective-permute-start(bf16[4,1,384,128]{3,2,1,0:T(8,128)(2,1)S(1)} %get-tuple-element.163), channel_id=1, source_target_pairs={{0,16},{16,0},{1,17},{17,1},{2,18},{18,2},{3,19},{19,3},{4,20},{20... | collective-permute-start | bytes 1179656 | tf_op jit(solution)/shard_map/ppermute | solution.py:25
  163.5 18.8 %collective-permute-start.33 = (bf16[4,1,384,128]{3,2,1,0:T(8,128)(2,1)S(1)}, bf16[4,1,384,128]{3,2,1,0:T(8,128)(2,1)S(1)}, u32[]{:S(2)}, u32[]{:S(2)}) collective-permute-start(bf16[4,1,384,128]{3,2,1,0:T(8,128)(2,1)S(1)} %get-tuple-element.165), channel_id=1, source_target_pairs={{0,2},{1,3},{2,0},{3,1},{4,6},{5,7},{6,4},{7,5},{8,10},{9,11},{10,... | collective-permute-start | bytes 1179656 | tf_op jit(solution)/shard_map/ppermute | solution.py:25
  168.4 21.2 %collective-permute-start.15 = (bf16[2,64,768]{2,1,0:T(8,128)(2,1)S(1)}, bf16[2,64,768]{2,1,0:T(8,128)(2,1)S(1)}, u32[]{:S(2)}, u32[]{:S(2)}) collective-permute-start(bf16[2,64,768]{2,1,0:T(8,128)(2,1)S(1)} %get-tuple-element.121), channel_id=1, source_target_pairs={{1,0},{2,1},{3,2},{4,3},{5,4},{6,5},{7,6},{8,7},{9,8},{10,9},{11,1... | collective-permute-start | bytes 589832 | tf_op jit(solution)/shard_map/ppermute | solution.py:31
  178.6 40.7 %collective-permute-start.24 = (bf16[256,384]{1,0:T(8,128)(2,1)S(1)}, bf16[256,384]{1,0:T(8,128)(2,1)S(1)}, u32[]{:S(2)}, u32[]{:S(2)}) collective-permute-start(bf16[256,384]{1,0:T(8,128)(2,1)S(1)} %get-tuple-element.142), channel_id=1, source_target_pairs={{0,16},{16,0},{1,17},{17,1},{2,18},{18,2},{3,19},{19,3},{4,20},{20... | collective-permute-start | bytes 589832 | tf_op jit(solution)/shard_map/ppermute | solution.py:25
  181.6 31.4 %collective-permute-start.25 = (bf16[192,1024]{1,0:T(8,128)(2,1)S(1)}, bf16[192,1024]{1,0:T(8,128)(2,1)S(1)}, u32[]{:S(2)}, u32[]{:S(2)}) collective-permute-start(bf16[192,1024]{1,0:T(8,128)(2,1)S(1)} %get-tuple-element.144), channel_id=1, source_target_pairs={{0,16},{16,0},{1,17},{17,1},{2,18},{18,2},{3,19},{19,3},{4,20},{20... | collective-permute-start | bytes 1179656 | tf_op jit(solution)/shard_map/ppermute | solution.py:25
  182.4 29.7 %collective-permute-start.19 = (bf16[4,1,240,128]{3,2,1,0:T(8,128)(2,1)S(1)}, bf16[4,1,240,128]{3,2,1,0:T(8,128)(2,1)S(1)}, u32[]{:S(2)}, u32[]{:S(2)}) collective-permute-start(bf16[4,1,240,128]{3,2,1,0:T(8,128)(2,1)S(1)} %get-tuple-element.131), channel_id=1, source_target_pairs={{0,16},{16,0},{1,17},{17,1},{2,18},{18,2},{3,19},{19,3},{4,20},{20... | collective-permute-start | bytes 737288 | tf_op jit(solution)/shard_map/ppermute | solution.py:25
  184.9 27.9 %collective-permute-start.20 = (bf16[4,1,240,128]{3,2,1,0:T(8,128)(2,1)S(1)}, bf16[4,1,240,128]{3,2,1,0:T(8,128)(2,1)S(1)}, u32[]{:S(2)}, u32[]{:S(2)}) collective-permute-start(bf16[4,1,240,128]{3,2,1,0:T(8,128)(2,1)S(1)} %get-tuple-element.133), channel_id=1, source_target_pairs={{0,2},{1,3},{2,0},{3,1},{4,6},{5,7},{6,4},{7,5},{8,10},{9,11},{10,... | collective-permute-start | bytes 737288 | tf_op jit(solution)/shard_map/ppermute | solution.py:25
  189.7 36.9 %collective-permute-start.34 = (bf16[2,1,768,128]{3,2,1,0:T(8,128)(2,1)S(1)}, bf16[2,1,768,128]{3,2,1,0:T(8,128)(2,1)S(1)}, u32[]{:S(2)}, u32[]{:S(2)}) collective-permute-start(bf16[2,1,768,128]{3,2,1,0:T(8,128)(2,1)S(1)} %get-tuple-element.167), channel_id=1, source_target_pairs={{0,4},{1,5},{2,6},{3,7},{4,0},{5,1},{6,2},{7,3},{8,12},{9,13},{10,... | collective-permute-start | bytes 1179656 | tf_op jit(solution)/shard_map/ppermute | solution.py:25
  212.9 13.5 %collective-permute-start.21 = (bf16[2,1,480,128]{3,2,1,0:T(8,128)(2,1)S(1)}, bf16[2,1,480,128]{3,2,1,0:T(8,128)(2,1)S(1)}, u32[]{:S(2)}, u32[]{:S(2)}) collective-permute-start(bf16[2,1,480,128]{3,2,1,0:T(8,128)(2,1)S(1)} %get-tuple-element.135), channel_id=1, source_target_pairs={{0,4},{1,5},{2,6},{3,7},{4,0},{5,1},{6,2},{7,3},{8,12},{9,13},{10,... | collective-permute-start | bytes 737288 | tf_op jit(solution)/shard_map/ppermute | solution.py:25
  226.6 16.7 %collective-permute-start.35 = (bf16[1,1,768,128]{3,2,1,0:T(8,128)(2,1)S(1)}, bf16[1,1,768,128]{3,2,1,0:T(8,128)(2,1)S(1)}, u32[]{:S(2)}, u32[]{:S(2)}) collective-permute-start(bf16[1,1,768,128]{3,2,1,0:T(8,128)(2,1)S(1)} %get-tuple-element.169), channel_id=1, source_target_pairs={{0,8},{1,9},{2,10},{3,11},{4,12},{5,13},{6,14},{7,15},{8,0},{9,1},... | collective-permute-start | bytes 589832 | tf_op jit(solution)/shard_map/ppermute | solution.py:25
  (31 other events, 239.0 us)
